TPU v7x, 512 devices: a whole 4x8x8 slice. The times are simulated.
512 devices in a mesh: row: 32 (over z, y_lo), col: 16 (over x, y_hi, core).
Axes of the slice: x: 4, y: 8 (y_hi: 2, y_lo: 4; y = y_hi * 4 + y_lo), z: 8, core: 2. Of those that a mesh axis runs over, the one named last changes fastest.
Arguments:
- grad_out: bfloat16 [65536, 512], P(('row', 'col')), may hold values from -6 to 6
- relu_mask: int32 [65536, 512], P(('row', 'col')), may hold values 0 or 1
- features: bfloat16 [65536, 512], P(('row', 'col')), may hold values from -6 to 6
- weight: bfloat16 [512, 512], replicated, may hold values from -0.25 to 0.25
- tile_vals: bfloat16 [32, 16, 96, 128, 128], P('row', 'col'), may hold values from -0.1796875 to 0.1796875
- tile_rows: int32 [32, 16, 96], P('row', 'col'), may hold values from 0 to 31, as said below
- tile_cols: int32 [32, 16, 96], P('row', 'col'), may hold values from 0 to 15, as said below
- tile_count: int32 [32, 16], P('row', 'col'), may hold values from 1 to 96, as said below
Outputs:
- grad_in: bfloat16 [65536, 512], P(('row', 'col'))
- grad_weight: float32 [512, 512], replicated
Inputs may be any that keep to these rules, and one draw needn't show every extreme that they name: `tile_rows`: within one block, the live slots name distinct pairs of tile row and tile column. `tile_cols`: within one block, the live slots name distinct pairs of tile row and tile column. `tile_count`: some block has all 96 slots live in every draw; loads are skewed over blocks.
All inputs are finite; a program needn't handle non-finite values. No bound on the sum of `relu_mask` on one device may be relied on, other than what follows from the above.
Results may differ from a plain program's by a relative error of at most 0.024.
Values may be sent and summed in bfloat16 or wider, within the bound.
No kernel may reach another device: no remote copies, remote signals or barrier semaphores. Data moves between devices by JAX's collectives and lax.ppermute only.
A program may use at most 64 MiB of HBM per device.

v0:
```python
import jax
import jax.numpy as jnp
from jax import lax
from jax.sharding import PartitionSpec as P

GROUP = 8


def tile_terms(values, rows, cols, count, source, turns, dst_tiles):

    def add_group(index, acc):
        start = index * GROUP
        group_vals = lax.dynamic_slice_in_dim(values, start, GROUP, 0)
        group_rows = lax.dynamic_slice_in_dim(rows, start, GROUP, 0)
        group_cols = lax.dynamic_slice_in_dim(cols, start, GROUP, 0)
        live = start + jnp.arange(GROUP, dtype=jnp.int32) < count
        pieces = source[group_cols]
        prod = jnp.einsum("kij,kjf->kif", group_vals, pieces, preferred_element_type=jnp.float32)
        prod = prod * live[:, None, None].astype(jnp.float32)
        return acc.at[group_rows].add(prod)

    empty = jnp.zeros((dst_tiles, source.shape[1], source.shape[2]), jnp.float32)
    total = lax.fori_loop(0, turns, add_group, empty)
    return total.astype(jnp.bfloat16).astype(jnp.float32)


def body(grad_out, relu_mask, features, weight, tile_vals, tile_rows, tile_cols, tile_count):
    slope = (grad_out.astype(jnp.float32) * relu_mask.astype(jnp.float32)).astype(jnp.bfloat16)
    gathered = lax.all_gather(slope, "col", axis=0, tiled=True)
    tile_side = tile_vals.shape[-1]
    width = slope.shape[1]
    source = gathered.reshape(-1, tile_side, width)
    dst_tiles = lax.axis_size("row") * slope.shape[0] // tile_side
    values = tile_vals[0, 0]
    rows = tile_rows[0, 0]
    cols = tile_cols[0, 0]
    count = tile_count[0, 0]
    turns = values.shape[0] // GROUP
    partial_terms = tile_terms(values, rows, cols, count, source, turns, dst_tiles)
    summed = lax.psum_scatter(
        partial_terms.astype(jnp.bfloat16), "row", scatter_dimension=0, tiled=True
    ).astype(jnp.float32)
    aggregated = summed.reshape(-1, width).astype(jnp.bfloat16)
    grad_in = lax.dot_general(
        aggregated, weight, (((1,), (1,)), ((), ())), preferred_element_type=jnp.float32
    ).astype(jnp.bfloat16)
    local_weight = lax.dot_general(
        features, aggregated, (((0,), (0,)), ((), ())), preferred_element_type=jnp.float32
    )
    grad_weight = lax.psum(local_weight, ("row", "col"))
    return (grad_in, grad_weight)


def solution(mesh):
    return jax.shard_map(
        body,
        mesh=mesh,
        in_specs=(
            P(("row", "col"), None),
            P(("row", "col"), None),
            P(("row", "col"), None),
            P(),
            P("row", "col", None, None, None),
            P("row", "col", None),
            P("row", "col", None),
            P("row", "col"),
        ),
        out_specs=(P(("row", "col"), None), P()),
        check_vma=False,
    )
```

profile of v0, /device:TPU:1, one launch (start us, length us, event | category | flops | bytes accessed | tf_op | source)
XLA Modules:
  0.0 671.8 jit_solution(1302162943684781984)
XLA Ops:
  9.0 75.3 %all-gather.2.cloned.1.call-done = bf16[2048,512]{1,0:T(8,128)(2,1)} async-done(((bf16[128,512]{1,0:T(8,128)(2,1)}), bf16[2048,512]{1,0:T(8,128)(2,1)}) %all-gather.2.cloned.1.call-update) | async-done | bytes 2097168 | tf_op jit(solution)/shard_map/all_gather | solution.py:29
  84.3 4.3 broadcast_in_dim.20
  88.7 119.7 %while.13 = (s32[]{:T(128)}, f32[32,128,512]{2,1,0:T(8,128)}, s32[96]{0:T(128)S(1)}, bf16[96,128,128]{2,1,0:T(8,128)(2,1)}, s32[96]{0:T(128)S(1)}, /*index=5*/bf...) while((s32[]{:T(128)}, f32[32,128,512]{2,1,0:T(8,128)}, ...), condition=%wide.region_2.0_spmd, body=%wide.region_0.0_spmd.sunk | while | flops 135267408 | bytes 11801035 | solution.py:23
  89.4 3.2 gather_fusion
  94.3 4.3 scatter_fusion
  99.4 3.2 gather_fusion
  104.3 4.3 scatter_fusion
  109.3 3.2 gather_fusion
  114.2 4.3 scatter_fusion
  119.3 3.2 gather_fusion
  124.2 4.3 scatter_fusion
  129.3 3.2 gather_fusion
  134.2 4.4 scatter_fusion
  139.4 3.2 gather_fusion
  144.3 4.3 scatter_fusion
  149.3 3.2 gather_fusion
  154.2 4.4 scatter_fusion
  159.3 3.2 gather_fusion
  164.2 4.2 scatter_fusion
  169.2 3.2 gather_fusion
  174.1 4.3 scatter_fusion
  179.1 3.2 gather_fusion
  184.0 4.3 scatter_fusion
  189.1 3.2 gather_fusion
  194.0 4.3 scatter_fusion
  199.1 3.2 gather_fusion
  204.0 4.4 scatter_fusion
  208.4 6.0 convert_element_type.37
  214.4 151.0 %reduce-scatter.2.cloned.1.call-done = bf16[1,128,512]{2,1,0:T(8,128)(2,1)} async-done(((bf16[32,128,512]{2,1,0:T(8,128)(2,1)}), bf16[1,128,512]{2,1,0:T(8,128)(2,1)}) %reduce-scatter.2.cloned.1.call-update) | async-done | bytes 131088 | tf_op jit(solution)/shard_map/reduce_scatter | solution.py:40
  365.4 2.2 convolution_bitcast_fusion
  369.5 293.2 %all-reduce.2.cloned.1.call-done = f32[512,512]{0,1:T(8,128)} async-done(((f32[512,512]{0,1:T(8,128)}), f32[512,512]{0,1:T(8,128)}) %all-reduce.2.cloned.1.call-update) | async-done | bytes 1048592 | tf_op jit(solution)/shard_map/psum | solution.py:50
  662.7 2.5 copy.10
  (64 shorter events, 33.4 us)
Async XLA Ops:
  7.2 360.5 %copy-start = (bf16[512,512]{1,0:T(8,128)(2,1)S(1)}, bf16[512,512]{1,0:T(8,128)(2,1)}, u32[]{:S(2)}) copy-start(bf16[512,512]{1,0:T(8,128)(2,1)} %param.13) | copy-start | bytes 1572868
  7.2 77.2 %all-gather.2.cloned.1.call-start = ((), (), s32[]{:S(2)}) async-start(), calls=%async_computation.1 | async-start | bytes 2228224 | tf_op jit(solution)/shard_map/all_gather | solution.py:29
  9.0 356.5 %reduce-scatter.2.cloned.1.call-start = ((), (), s32[]{:S(2)}) async-start(), calls=%async_computation.2 | async-start | bytes 4325376 | tf_op jit(solution)/shard_map/reduce_scatter | solution.py:40
  84.3 4.3 copy-start.2
  84.3 4.3 copy-start.3
  214.3 151.1 %copy-start.1 = (bf16[128,512]{1,0:T(8,128)(2,1)S(1)}, bf16[128,512]{1,0:T(8,128)(2,1)}, u32[]{:S(2)}) copy-start(bf16[128,512]{1,0:T(8,128)(2,1)} %param.12) | copy-start | bytes 393220
  214.4 448.4 %all-reduce.2.cloned.1.call-start = ((), (), s32[]{:S(2)}) async-start(), calls=%async_computation.3 | async-start | bytes 2097152 | tf_op jit(solution)/shard_map/psum | solution.py:50
Sparse Core Ops, SparseCore 0:
  11.9 72.4 all-gather.1
  214.5 150.9 reduce-scatter.1
  371.1 291.6 all-reduce.1
where the time goes:
time: 673 us; the launch traced here: 672 us
  waiting for transfers between devices  520 us (77%)
  other arithmetic  68.4 us (10%)
  local copies, waits for them, and re-layouts  44.9 us (7%)
  matrix products  24.8 us (4%)
  between operations  13.8 us (2%)
    psum x1, waiting for transfers between devices, body(): grad_weight = lax.psum(local_weight, ('row', 'col'))  293 us
    reduce_scatter x1, waiting for transfers between devices, body(): lax.psum_scatter(partial_terms.astype(jnp.bfloat16), 'row', scatter_dimen...  151 us
    all_gather x1, waiting for transfers between devices, body(): gathered = lax.all_gather(slope, 'col', axis=0, tiled=True)  75.3 us
    scatter-add x12, other arithmetic, add_group(): return acc.at[group_rows].add(prod)  51.8 us
    gather x12, local copies, waits for them, and re-layouts, add_group(): pieces = source[group_cols]  38.1 us
    dot_general x12, matrix products, add_group(): jnp.einsum('kij,kjf->kif', group_vals, pieces, preferred_element_type=jnp...  20.8 us
  transfers between devices with their start and end apart: 3, of which 3 were waited for; matrix products, arithmetic and copies ran while one was open for 0% of the time, Pallas kernels for 0%

commit v1 on v0

v1 whole, which is shorter than its diff:
```python
import jax
import jax.numpy as jnp
import numpy as np
from jax import lax
from jax.experimental import pallas as pl
from jax.experimental.pallas import tpu as pltpu
from jax.sharding import Mesh, PartitionSpec as P

SIZES = (8, 4, 4, 2, 2)
AXES = ("z", "y", "x", "h", "k")
UNROLL = 8
VMEM_LIMIT = 48 << 20

SMEM_SPEC = pl.BlockSpec(memory_space=pltpu.SMEM)
VMEM_SPEC = pl.BlockSpec(memory_space=pltpu.VMEM)


def permute(value, move):
    pairs = []
    for index, place in enumerate(np.ndindex(*SIZES)):
        pairs.append((index, int(np.ravel_multi_index(move(*place), SIZES))))
    return lax.ppermute(value, AXES, pairs)


def h_swap(z, y, x, h, k):
    return (z, y, x, 1 - h, k)


def k_swap(z, y, x, h, k):
    return (z, y, x, h, 1 - k)


def x_from(step):
    def move(z, y, x, h, k):
        return (z, y, (x - step) % 4, h, k)

    return move


def kernel_call(kernel, out_shape, in_specs, scratch=(), name=None):
    return pl.pallas_call(
        kernel,
        out_shape=out_shape,
        in_specs=in_specs,
        out_specs=jax.tree.map(lambda _: VMEM_SPEC, out_shape),
        scratch_shapes=list(scratch),
        compiler_params=pltpu.CompilerParams(vmem_limit_bytes=VMEM_LIMIT),
        name=name,
    )


def block_kernel(count, rows, places, vals, own, other, out, acc, source):
    source[0:8] = own[...]
    source[8:16] = other[...]
    acc[...] = jnp.zeros_like(acc)
    live = count[0]

    def group(index, carry):
        terms = []
        for step in range(UNROLL):
            slot = index * UNROLL + step
            place = places[slot]
            term = jnp.dot(vals[slot], source[place], preferred_element_type=jnp.float32)
            terms.append((rows[slot], jnp.where(slot < live, term, 0.0)))
        for row, term in terms:
            acc[row] += term
        return carry

    lax.fori_loop(0, pl.cdiv(live, UNROLL), group, 0)
    out[...] = acc[...].astype(jnp.bfloat16)


def node_kernel(parts, weight, grad_in, agg_t):
    total = parts[0].astype(jnp.float32)
    for index in range(1, 4):
        total = total + parts[index].astype(jnp.float32)
    agg = total.astype(jnp.bfloat16)
    grad_in[...] = lax.dot_general(
        agg, weight[...], (((1,), (1,)), ((), ())), preferred_element_type=jnp.float32
    ).astype(jnp.bfloat16)
    agg_t[...] = agg.astype(jnp.float32).T.astype(jnp.bfloat16).reshape(8, 64, 128)


def slice_kernel(agg_t, features, out):
    total = jnp.zeros((64, 512), jnp.float32)
    for index in range(8):
        total += jnp.dot(agg_t[index], features[index], preferred_element_type=jnp.float32)
    for index in range(4):
        out[:, index, :] = total[:, 128 * index:128 * (index + 1)]


def sum_kernel(parts, out):
    total = jnp.sum(parts[...], axis=0)
    out[...] = jnp.broadcast_to(total[None], out.shape)


def last_kernel(at, own, other, out, whole):
    x, k = at[0], at[1]
    for step in range(4):
        chip = lax.rem(x + step, 4)
        whole[chip * 2 + k] = own[step]
        whole[chip * 2 + 1 - k] = other[step]
    out[...] = whole[...].reshape(512, 512).astype(jnp.float32).T


def body(grad_out, relu_mask, features, weight, tile_vals, tile_rows, tile_cols, tile_count):
    x, h, k = (lax.axis_index(name) for name in ("x", "h", "k"))
    slope = (grad_out.astype(jnp.float32) * relu_mask.astype(jnp.float32)).astype(jnp.bfloat16)

    pair = jnp.stack([slope, permute(slope, h_swap)])
    own = jnp.concatenate([pair] + [permute(pair, x_from(step)) for step in (1, 2, 3)])
    other = permute(own, k_swap)
    cols = tile_cols[0, 0]
    places = ((cols // 4 - x) % 4) * 2 + ((cols // 2 % 2) ^ h) + 8 * ((cols % 2) ^ k)

    terms = kernel_call(
        block_kernel,
        jax.ShapeDtypeStruct((32, 128, 512), jnp.bfloat16),
        [SMEM_SPEC] * 3 + [VMEM_SPEC] * 3,
        [pltpu.VMEM((32, 128, 512), jnp.float32), pltpu.VMEM((16, 128, 512), jnp.bfloat16)],
        name="block_terms",
    )(tile_count[0], tile_rows[0, 0], places, tile_vals[0, 0], own, other)

    parts = lax.psum_scatter(terms, "z", scatter_dimension=0, tiled=True)
    parts = lax.all_to_all(parts, "y", 0, 0, tiled=True)
    grad_in, agg_t = kernel_call(
        node_kernel,
        (jax.ShapeDtypeStruct((128, 512), jnp.bfloat16), jax.ShapeDtypeStruct((8, 64, 128), jnp.bfloat16)),
        [VMEM_SPEC] * 2,
        name="nodes",
    )(parts, weight)

    gathered = lax.all_gather(features, ("x", "k"), axis=0, tiled=False)
    agg_t = lax.all_to_all(agg_t, ("x", "k"), 0, 0, tiled=True)
    share = kernel_call(
        slice_kernel, jax.ShapeDtypeStruct((64, 4, 128), jnp.float32), [VMEM_SPEC] * 2, name="weight_slice"
    )(agg_t, gathered)
    share = lax.all_to_all(share, ("z", "y", "h"), 0, 0, tiled=True)
    share = kernel_call(
        sum_kernel, jax.ShapeDtypeStruct((64, 4, 128), jnp.float32), [VMEM_SPEC], name="weight_sum"
    )(share)
    share = lax.all_to_all(share, ("z", "y", "h"), 0, 0, tiled=True)
    share = share.reshape(1, 64, 512).astype(jnp.bfloat16)
    own = jnp.concatenate([share] + [permute(share, x_from(step)) for step in (1, 2, 3)])
    other = permute(own, k_swap)
    grad_weight = kernel_call(
        last_kernel,
        jax.ShapeDtypeStruct((512, 512), jnp.float32),
        [SMEM_SPEC] + [VMEM_SPEC] * 2,
        [pltpu.VMEM((8, 64, 512), jnp.bfloat16)],
        name="weight_order",
    )(jnp.stack([x, k]), own, other)
    return (grad_in, grad_weight)


def solution(mesh):
    fine = Mesh(mesh.devices.reshape(SIZES), AXES)
    nodes = P(AXES, None)
    rows, cols = AXES[:2], AXES[2:]
    return jax.shard_map(
        body,
        mesh=fine,
        in_specs=(
            nodes,
            nodes,
            nodes,
            P(),
            P(rows, cols, None, None, None),
            P(rows, cols, None),
            P(rows, cols, None),
            P(rows, cols),
        ),
        out_specs=(nodes, P()),
        check_vma=False,
    )
```

time: 673 us -> 216 us (0.32)
  waiting for transfers between devices: 520 us -> 87.4 us
  other arithmetic: 68.4 us -> 1.83 us
  blocking collectives: 0 us -> 53.6 us
  starting transfers between devices: 0.12 us -> 45 us
  local copies, waits for them, and re-layouts: 44.9 us -> 3.89 us
  matrix products: 24.8 us -> 0 us
  Pallas kernels: 0 us -> 7.18 us
    psum x1 -> x0, waiting for transfers between devices: 293 us -> none  [body(): grad_weight = lax.psum(local_weight, ('row', 'col'))]
    reduce_scatter x1, waiting for transfers between devices: 151 us -> 63.7 us  [body(): parts = lax.psum_scatter(terms, 'z', scatter_dimension=0, tiled=True)]
    all_gather x1, waiting for transfers between devices: 75.3 us -> 0.01 us  [body(): gathered = lax.all_gather(features, ('x', 'k'), axis=0, tiled=False)]
    all_to_all x0 -> x3, blocking collectives: none -> 53.6 us  [the longest x2 35.6 us: body(): share = lax.all_to_all(share, ('z', 'y', 'h'), 0, 0, tiled=True)]
    scatter-add x12 -> x0, other arithmetic: 51.8 us -> none  [add_group(): return acc.at[group_rows].add(prod)]
    ppermute x0 -> x9, starting transfers between devices: none -> 38.9 us  [permute(): return lax.ppermute(value, AXES, pairs)]
    gather x12 -> x0, local copies, waits for them, and re-layouts: 38.1 us -> none  [add_group(): pieces = source[group_cols]]
    dot_general x14 -> x0, matrix products: 24.8 us -> none  [the longest x12 20.8 us: add_group(): jnp.einsum('kij,kjf->kif', group_vals, pieces, preferred_element_type=jnp...]
  transfers between devices with their start and end apart: 3 -> 12, of which waited for: 3 -> 9; matrix products, arithmetic and copies ran while one was open for 0% -> 0% of each run, Pallas kernels for 0% -> 0%
where the time goes in v1:
time: 216 us; the launch traced here: 215 us
  waiting for transfers between devices  87.4 us (40%)
  blocking collectives  53.6 us (25%)
  starting transfers between devices  45 us (21%)
  between operations  16.3 us (8%)
  Pallas kernels  7.18 us (3%)
  local copies, waits for them, and re-layouts  3.89 us (2%)
    reduce_scatter x1, waiting for transfers between devices, body(): parts = lax.psum_scatter(terms, 'z', scatter_dimension=0, tiled=True)  63.7 us
    ppermute x9, starting transfers between devices, permute(): return lax.ppermute(value, AXES, pairs)  38.9 us
    all_to_all x2, blocking collectives, body(): share = lax.all_to_all(share, ('z', 'y', 'h'), 0, 0, tiled=True)  35.6 us
    all_to_all x1, blocking collectives, body(): parts = lax.all_to_all(parts, 'y', 0, 0, tiled=True)  18 us
    ppermute x9, waiting for transfers between devices, permute(): return lax.ppermute(value, AXES, pairs)  18 us
    all_to_all x1, starting transfers between devices, body(): agg_t = lax.all_to_all(agg_t, ('x', 'k'), 0, 0, tiled=True)  6 us
    all_to_all x1, waiting for transfers between devices, body(): agg_t = lax.all_to_all(agg_t, ('x', 'k'), 0, 0, tiled=True)  5.27 us
  transfers between devices with their start and end apart: 12, of which 9 were waited for; matrix products, arithmetic and copies ran while one was open for 0% of the time, Pallas kernels for 0%

profile of v1, /device:TPU:1, one launch (start us, length us, event | category | flops | bytes accessed | tf_op | source)
XLA Modules:
  0.0 215.3 jit_solution(7465497138842290453)
XLA Ops:
  8.0 1.0 constant_dynamic-update-slice_fusion.4
  9.1 8.3 %collective-permute-start = (bf16[128,512]{1,0:T(8,128)(2,1)S(1)}, bf16[128,512]{1,0:T(8,128)(2,1)S(1)}, u32[]{:S(2)}, u32[]{:S(2)}) collective-permute-start(bf16[128,512]{1,0:T(8,128)(2,1)S(1)} %get-tuple-element.7), channel_id=1, source_target_pairs={{0,2},{1,3},{2,0},{3,1},{4,6},{5,7},{6,4},{7,5},{8,10},{9,11},{10,... | collective-permute-start | bytes 393224 | tf_op jit(solution)/shard_map/ppermute | solution.py:22
  17.4 4.9 %collective-permute-done = bf16[128,512]{1,0:T(8,128)(2,1)S(1)} collective-permute-done((bf16[128,512]{1,0:T(8,128)(2,1)S(1)}, bf16[128,512]{1,0:T(8,128)(2,1)S(1)}, u32[]{:S(2)}, u32[]{:S(2)}) %collective-permute-start) | collective-permute-done | bytes 131104 | tf_op jit(solution)/shard_map/ppermute | solution.py:22
  22.2 2.6 %collective-permute-start.1 = (bf16[2,128,512]{2,1,0:T(8,128)(2,1)S(1)}, bf16[2,128,512]{2,1,0:T(8,128)(2,1)S(1)}, u32[]{:S(2)}, u32[]{:S(2)}) collective-permute-start(bf16[2,128,512]{2,1,0:T(8,128)(2,1)S(1)} %pad_maximum_fusion), channel_id=1, source_target_pairs={{0,12},{1,13},{2,14},{3,15},{4,0},{5,1},{6,2},{7,3},{8,4},{9,5},{1... | collective-permute-start | bytes 786440 | tf_op jit(solution)/shard_map/ppermute | solution.py:22
  24.9 2.4 %collective-permute-start.2 = (bf16[2,128,512]{2,1,0:T(8,128)(2,1)S(1)}, bf16[2,128,512]{2,1,0:T(8,128)(2,1)S(1)}, u32[]{:S(2)}, u32[]{:S(2)}) collective-permute-start(bf16[2,128,512]{2,1,0:T(8,128)(2,1)S(1)} %pad_maximum_fusion), channel_id=1, source_target_pairs={{0,8},{1,9},{2,10},{3,11},{4,12},{5,13},{6,14},{7,15},{8,0},{9,1},... | collective-permute-start | bytes 786440 | tf_op jit(solution)/shard_map/ppermute | solution.py:22
  27.3 2.5 %collective-permute-start.3 = (bf16[2,128,512]{2,1,0:T(8,128)(2,1)S(1)}, bf16[2,128,512]{2,1,0:T(8,128)(2,1)S(1)}, u32[]{:S(2)}, u32[]{:S(2)}) collective-permute-start(bf16[2,128,512]{2,1,0:T(8,128)(2,1)S(1)} %pad_maximum_fusion), channel_id=1, source_target_pairs={{0,4},{1,5},{2,6},{3,7},{4,8},{5,9},{6,10},{7,11},{8,12},{9,13},{1... | collective-permute-start | bytes 786440 | tf_op jit(solution)/shard_map/ppermute | solution.py:22
  29.9 3.7 %collective-permute-done.2 = bf16[2,128,512]{2,1,0:T(8,128)(2,1)S(1)} collective-permute-done((bf16[2,128,512]{2,1,0:T(8,128)(2,1)S(1)}, bf16[2,128,512]{2,1,0:T(8,128)(2,1)S(1)}, u32[]{:S(2)}, u32[]{:S(2)}) %collective-permute-start.2) | collective-permute-done | bytes 262176 | tf_op jit(solution)/shard_map/ppermute | solution.py:22
  33.6 3.2 %collective-permute-done.3 = bf16[2,128,512]{2,1,0:T(8,128)(2,1)S(1)} collective-permute-done((bf16[2,128,512]{2,1,0:T(8,128)(2,1)S(1)}, bf16[2,128,512]{2,1,0:T(8,128)(2,1)S(1)}, u32[]{:S(2)}, u32[]{:S(2)}) %collective-permute-start.3) | collective-permute-done | bytes 262176 | tf_op jit(solution)/shard_map/ppermute | solution.py:22
  36.8 8.2 %collective-permute-start.4 = (bf16[8,128,512]{2,1,0:T(8,128)(2,1)S(1)}, bf16[8,128,512]{2,1,0:T(8,128)(2,1)S(1)}, u32[]{:S(2)}, u32[]{:S(2)}) collective-permute-start(bf16[8,128,512]{2,1,0:T(8,128)(2,1)S(1)} %constant_dynamic-update-slice_fusion.own), channel_id=1, source_target_pairs={{0,1},{1,0},{2,3},{3,2},{4,5},{5,4},{6,7},{7,6},{8,9},{9,8},{10,11... | collective-permute-start | bytes 3145736 | tf_op jit(solution)/shard_map/ppermute | solution.py:22
  45.7 0.7 fusion.2.places
  46.4 0.9 collective-permute-done.4.other
  47.3 1.9 copy-done
  49.2 0.7 copy-done.3
  49.8 4.0 %block_terms.1 = bf16[32,128,512]{2,1,0:T(8,128)(2,1)} custom-call(s32[1]{0:T(128)} %bitcast.26.count, s32[96]{0:T(128)S(1)} %bitcast.29, s32[96]{0:T(128)S(1)} %fusion.2.places, bf16[96,128,128]{2,1,0:T(8,128)(2,1)S(1)} %bitcast.27, bf16[8,128,512]{2,1,0:T(8,128)(2,1)S(1)} %constant_dynamic-update-slice_fusion.own, ...), custom_call_target="tpu_custom_call" | custom-call | tf_op jit(solution)/shard_map/block_terms/pallas_call | solution.py:116
  53.9 0.5 all-gather.3.cloned.1.call-update
  54.4 63.7 %reduce-scatter.2.cloned.1.call-done = bf16[4,128,512]{2,1,0:T(8,128)(2,1)} async-done(((bf16[32,128,512]{2,1,0:T(8,128)(2,1)}), bf16[4,128,512]{2,1,0:T(8,128)(2,1)}) %reduce-scatter.2.cloned.1.call-update) | async-done | bytes 524304 | tf_op jit(solution)/shard_map/reduce_scatter | solution.py:124
  118.1 18.0 %all_to_all.20.parts = bf16[4,128,512]{2,1,0:T(8,128)(2,1)S(1)} all-to-all(bf16[4,128,512]{2,1,0:T(8,128)(2,1)} %reduce-scatter.2.cloned.1.call-done), channel_id=1, replica_groups=mesh['z'=8,'y'=4,'x'=4,'h'=2,'k'=2] {'y'}, dimensions={0} | all-to-all | bytes 1048576 | tf_op jit(solution)/shard_map/all_to_all | solution.py:125
  136.1 1.0 nodes.1
  137.1 6.0 %all-to-all-start.1 = ((bf16[8,64,128]{2,1,0:T(8,128)(2,1)}), bf16[8,64,128]{2,1,0:T(8,128)(2,1)S(1)}, u32[]{:S(2)}, u32[]{:S(2)}) async-start(bf16[8,64,128]{2,1,0:T(8,128)(2,1)} %get-tuple-element.5), calls=%async_computation.2 | async-start | bytes 262144 | tf_op jit(solution)/shard_map/all_to_all | solution.py:134
  143.1 5.3 %all-to-all-done.1.agg_t = bf16[8,64,128]{2,1,0:T(8,128)(2,1)S(1)} async-done(((bf16[8,64,128]{2,1,0:T(8,128)(2,1)}), bf16[8,64,128]{2,1,0:T(8,128)(2,1)S(1)}, u32[]{:S(2)}, u32[]{:S(2)}) %all-to-all-start.1) | async-done | bytes 131104 | tf_op jit(solution)/shard_map/all_to_all | solution.py:134
  148.4 1.2 copy-done.1
  149.6 0.3 weight_slice.1
  150.0 20.6 %all_to_all.21.parts = f32[64,4,128]{2,1,0:T(4,128)S(1)} all-to-all(f32[64,4,128]{2,1,0:T(4,128)S(1)} %weight_slice.1), channel_id=1, replica_groups=mesh['z'=8,'y'=4,'x'=4,'h'=2,'k'=2] {'z','y','h'}, dimensions={0} | all-to-all | bytes 262144 | tf_op jit(solution)/shard_map/all_to_all | solution.py:138
  170.7 15.0 %all_to_all.22 = bf16[64,4,128]{2,1,0:T(4,128)(2,1)S(1)} all-to-all(bf16[64,4,128]{2,1,0:T(4,128)(2,1)S(1)} %convert), channel_id=1, replica_groups=mesh['z'=8,'y'=4,'x'=4,'h'=2,'k'=2] {'z','y','h'}, dimensions={0} | all-to-all | bytes 131072 | tf_op jit(solution)/shard_map/all_to_all | solution.py:142
  185.7 2.8 %collective-permute-start.5 = (bf16[1,64,512]{2,1,0:T(8,128)(2,1)S(1)}, bf16[1,64,512]{2,1,0:T(8,128)(2,1)S(1)}, u32[]{:S(2)}, u32[]{:S(2)}) collective-permute-start(bf16[1,64,512]{2,1,0:T(8,128)(2,1)S(1)} %convert_element_type.27), channel_id=1, source_target_pairs={{0,12},{1,13},{2,14},{3,15},{4,0},{5,1},{6,2},{7,3},{8,4},{9,5},{1... | collective-permute-start | bytes 196616 | tf_op jit(solution)/shard_map/ppermute | solution.py:22
  188.5 3.1 %collective-permute-start.6 = (bf16[1,64,512]{2,1,0:T(8,128)(2,1)S(1)}, bf16[1,64,512]{2,1,0:T(8,128)(2,1)S(1)}, u32[]{:S(2)}, u32[]{:S(2)}) collective-permute-start(bf16[1,64,512]{2,1,0:T(8,128)(2,1)S(1)} %convert_element_type.27), channel_id=1, source_target_pairs={{0,8},{1,9},{2,10},{3,11},{4,12},{5,13},{6,14},{7,15},{8,0},{9,1},... | collective-permute-start | bytes 196616 | tf_op jit(solution)/shard_map/ppermute | solution.py:22
  191.6 1.9 collective-permute-start.7
  193.6 1.4 collective-permute-done.6
  195.1 2.8 %collective-permute-done.7 = bf16[1,64,512]{2,1,0:T(8,128)(2,1)S(1)} collective-permute-done((bf16[1,64,512]{2,1,0:T(8,128)(2,1)S(1)}, bf16[1,64,512]{2,1,0:T(8,128)(2,1)S(1)}, u32[]{:S(2)}, u32[]{:S(2)}) %collective-permute-start.7) | collective-permute-done | bytes 65568 | tf_op jit(solution)/shard_map/ppermute | solution.py:22
  197.9 7.1 %collective-permute-start.8 = (bf16[4,64,512]{2,1,0:T(8,128)(2,1)S(1)}, bf16[4,64,512]{2,1,0:T(8,128)(2,1)S(1)}, u32[]{:S(2)}, u32[]{:S(2)}) collective-permute-start(bf16[4,64,512]{2,1,0:T(8,128)(2,1)S(1)} %constant_dynamic-update-slice_fusion.5.own), channel_id=1, source_target_pairs={{0,1},{1,0},{2,3},{3,2},{4,5},{5,4},{6,7},{7,6},{8,9},{9,8},{10,11... | collective-permute-start | bytes 786440 | tf_op jit(solution)/shard_map/ppermute | solution.py:22
  205.0 1.1 collective-permute-done.8.other
  206.1 1.8 weight_order.1
  (24 shorter events, 0.5 us)
Async XLA Ops:
  8.0 110.1 %reduce-scatter.2.cloned.1.call-start = ((), (), s32[]{:S(2)}) async-start(), calls=%async_computation.5 | async-start | bytes 4718592 | tf_op jit(solution)/shard_map/reduce_scatter | solution.py:124
  9.1 13.2 %collective-permute-start = (bf16[128,512]{1,0:T(8,128)(2,1)S(1)}, bf16[128,512]{1,0:T(8,128)(2,1)S(1)}, u32[]{:S(2)}, u32[]{:S(2)}) collective-permute-start(bf16[128,512]{1,0:T(8,128)(2,1)S(1)} %get-tuple-element.7), channel_id=1, source_target_pairs={{0,2},{1,3},{2,0},{3,1},{4,6},{5,7},{6,4},{7,5},{8,10},{9,11},{10,... | collective-permute-start | bytes 393224 | tf_op jit(solution)/shard_map/ppermute | solution.py:22
  22.2 7.6 %collective-permute-start.1 = (bf16[2,128,512]{2,1,0:T(8,128)(2,1)S(1)}, bf16[2,128,512]{2,1,0:T(8,128)(2,1)S(1)}, u32[]{:S(2)}, u32[]{:S(2)}) collective-permute-start(bf16[2,128,512]{2,1,0:T(8,128)(2,1)S(1)} %pad_maximum_fusion), channel_id=1, source_target_pairs={{0,12},{1,13},{2,14},{3,15},{4,0},{5,1},{6,2},{7,3},{8,4},{9,5},{1... | collective-permute-start | bytes 786440 | tf_op jit(solution)/shard_map/ppermute | solution.py:22
  24.9 8.7 %collective-permute-start.2 = (bf16[2,128,512]{2,1,0:T(8,128)(2,1)S(1)}, bf16[2,128,512]{2,1,0:T(8,128)(2,1)S(1)}, u32[]{:S(2)}, u32[]{:S(2)}) collective-permute-start(bf16[2,128,512]{2,1,0:T(8,128)(2,1)S(1)} %pad_maximum_fusion), channel_id=1, source_target_pairs={{0,8},{1,9},{2,10},{3,11},{4,12},{5,13},{6,14},{7,15},{8,0},{9,1},... | collective-permute-start | bytes 786440 | tf_op jit(solution)/shard_map/ppermute | solution.py:22
  27.3 9.4 %collective-permute-start.3 = (bf16[2,128,512]{2,1,0:T(8,128)(2,1)S(1)}, bf16[2,128,512]{2,1,0:T(8,128)(2,1)S(1)}, u32[]{:S(2)}, u32[]{:S(2)}) collective-permute-start(bf16[2,128,512]{2,1,0:T(8,128)(2,1)S(1)} %pad_maximum_fusion), channel_id=1, source_target_pairs={{0,4},{1,5},{2,6},{3,7},{4,8},{5,9},{6,10},{7,11},{8,12},{9,13},{1... | collective-permute-start | bytes 786440 | tf_op jit(solution)/shard_map/ppermute | solution.py:22
  36.8 10.5 %collective-permute-start.4 = (bf16[8,128,512]{2,1,0:T(8,128)(2,1)S(1)}, bf16[8,128,512]{2,1,0:T(8,128)(2,1)S(1)}, u32[]{:S(2)}, u32[]{:S(2)}) collective-permute-start(bf16[8,128,512]{2,1,0:T(8,128)(2,1)S(1)} %constant_dynamic-update-slice_fusion.own), channel_id=1, source_target_pairs={{0,1},{1,0},{2,3},{3,2},{4,5},{5,4},{6,7},{7,6},{8,9},{9,8},{10,11... | collective-permute-start | bytes 3145736 | tf_op jit(solution)/shard_map/ppermute | solution.py:22
  47.3 1.9 copy-start
  49.2 0.7 copy-start.3
  53.8 82.3 %copy-start.2 = (bf16[512,512]{1,0:T(8,128)(2,1)S(1)}, bf16[512,512]{1,0:T(8,128)(2,1)}, u32[]{:S(2)}) copy-start(bf16[512,512]{1,0:T(8,128)(2,1)} %weight.1) | copy-start | bytes 1572868
  53.9 89.2 %all-gather.3.cloned.1.call-start = ((), (), s32[]{:S(2)}) async-start(), calls=%async_computation.6 | async-start | bytes 1179648 | tf_op jit(solution)/shard_map/all_gather | solution.py:133
  137.1 11.3 %all-to-all-start.1 = ((bf16[8,64,128]{2,1,0:T(8,128)(2,1)}), bf16[8,64,128]{2,1,0:T(8,128)(2,1)S(1)}, u32[]{:S(2)}, u32[]{:S(2)}) async-start(bf16[8,64,128]{2,1,0:T(8,128)(2,1)} %get-tuple-element.5), calls=%async_computation.2 | async-start | bytes 262144 | tf_op jit(solution)/shard_map/all_to_all | solution.py:134
  148.4 1.2 copy-start.1
  185.7 7.8 %collective-permute-start.5 = (bf16[1,64,512]{2,1,0:T(8,128)(2,1)S(1)}, bf16[1,64,512]{2,1,0:T(8,128)(2,1)S(1)}, u32[]{:S(2)}, u32[]{:S(2)}) collective-permute-start(bf16[1,64,512]{2,1,0:T(8,128)(2,1)S(1)} %convert_element_type.27), channel_id=1, source_target_pairs={{0,12},{1,13},{2,14},{3,15},{4,0},{5,1},{6,2},{7,3},{8,4},{9,5},{1... | collective-permute-start | bytes 196616 | tf_op jit(solution)/shard_map/ppermute | solution.py:22
  188.5 6.5 %collective-permute-start.6 = (bf16[1,64,512]{2,1,0:T(8,128)(2,1)S(1)}, bf16[1,64,512]{2,1,0:T(8,128)(2,1)S(1)}, u32[]{:S(2)}, u32[]{:S(2)}) collective-permute-start(bf16[1,64,512]{2,1,0:T(8,128)(2,1)S(1)} %convert_element_type.27), channel_id=1, source_target_pairs={{0,8},{1,9},{2,10},{3,11},{4,12},{5,13},{6,14},{7,15},{8,0},{9,1},... | collective-permute-start | bytes 196616 | tf_op jit(solution)/shard_map/ppermute | solution.py:22
  191.6 6.2 %collective-permute-start.7 = (bf16[1,64,512]{2,1,0:T(8,128)(2,1)S(1)}, bf16[1,64,512]{2,1,0:T(8,128)(2,1)S(1)}, u32[]{:S(2)}, u32[]{:S(2)}) collective-permute-start(bf16[1,64,512]{2,1,0:T(8,128)(2,1)S(1)} %convert_element_type.27), channel_id=1, source_target_pairs={{0,4},{1,5},{2,6},{3,7},{4,8},{5,9},{6,10},{7,11},{8,12},{9,13},{1... | collective-permute-start | bytes 196616 | tf_op jit(solution)/shard_map/ppermute | solution.py:22
  197.9 8.2 %collective-permute-start.8 = (bf16[4,64,512]{2,1,0:T(8,128)(2,1)S(1)}, bf16[4,64,512]{2,1,0:T(8,128)(2,1)S(1)}, u32[]{:S(2)}, u32[]{:S(2)}) collective-permute-start(bf16[4,64,512]{2,1,0:T(8,128)(2,1)S(1)} %constant_dynamic-update-slice_fusion.5.own), channel_id=1, source_target_pairs={{0,1},{1,0},{2,3},{3,2},{4,5},{5,4},{6,7},{7,6},{8,9},{9,8},{10,11... | collective-permute-start | bytes 786440 | tf_op jit(solution)/shard_map/ppermute | solution.py:22
Sparse Core Ops, SparseCore 0:
  54.0 64.0 reduce-scatter.1
Sparse Core Ops, SparseCore 1:
  56.5 34.2 all-gather.2

commit v2 on v1

v2 whole, which is shorter than its diff:
```python
import functools

import jax
import jax.numpy as jnp
import numpy as np
from jax import lax
from jax.experimental import pallas as pl
from jax.experimental.pallas import tpu as pltpu
from jax.sharding import Mesh, PartitionSpec as P

SIZES = (8, 4, 4, 2, 2)
AXES = ("z", "y", "x", "h", "k")
UNROLL = 24
SLOTS = 96
HALF = 64
WIDTH = 512
VMEM_LIMIT = 16 << 20
VMEM_WHOLE = 48 << 20

SMEM_SPEC = pl.BlockSpec(memory_space=pltpu.SMEM)
VMEM_SPEC = pl.BlockSpec(memory_space=pltpu.VMEM)


def permute(value, move):
    pairs = []
    for index, place in enumerate(np.ndindex(*SIZES)):
        pairs.append((index, int(np.ravel_multi_index(move(*place), SIZES))))
    return lax.ppermute(value, AXES, pairs)


def h_swap(z, y, x, h, k):
    return (z, y, x, 1 - h, k)


def k_swap(z, y, x, h, k):
    return (z, y, x, h, 1 - k)


def x_from(step):
    def move(z, y, x, h, k):
        return (z, y, (x - step) % 4, h, k)

    return move


def y_from(step):
    def move(z, y, x, h, k):
        return (z, (y - step) % 4, x, h, k)

    return move


def y_flip(bit):
    def move(z, y, x, h, k):
        return (z, y ^ bit, x, h, k)

    return move


def z_up(z, y, x, h, k):
    return ((z + 1) % 8, y, x, h, k)


def z_down(z, y, x, h, k):
    return ((z - 1) % 8, y, x, h, k)


def kernel_call(kernel, out_shape, in_specs, scratch=(), name=None, limit=VMEM_LIMIT, out_specs=None):
    return pl.pallas_call(
        kernel,
        out_shape=out_shape,
        in_specs=in_specs,
        out_specs=out_specs or jax.tree.map(lambda _: VMEM_SPEC, out_shape),
        scratch_shapes=list(scratch),
        compiler_params=pltpu.CompilerParams(vmem_limit_bytes=limit),
        name=name,
    )


def block_kernel(at, codes, vals, own, own_h, other, other_h, *refs):
    pieces, (acc, source, held, sem) = refs[:9], refs[9:]
    copy = pltpu.make_async_copy(vals, held, sem)
    copy.start()
    for index, blocks in enumerate((own, own_h, other, other_h)):
        source[4 * index:4 * index + 4] = blocks[...]
    acc[...] = jnp.zeros_like(acc)
    copy.wait()

    def group(index, carry):
        terms = []
        for step in range(UNROLL):
            slot = index * UNROLL + step
            code = codes[slot]
            term = jnp.dot(held[slot], source[code % 16], preferred_element_type=jnp.float32)
            terms.append((code // 16, term))
        for row, term in terms:
            acc[row] += term
        return carry

    lax.fori_loop(0, pl.cdiv(codes[SLOTS], UNROLL), group, 0)

    def chunk(step, rows=slice(None)):
        return acc[pl.ds(4 * lax.rem(at[0] + step, 8), 4), rows].astype(jnp.bfloat16)

    pieces[0][...] = chunk(4, slice(0, HALF))
    pieces[1][...] = chunk(4, slice(HALF, 128))
    for piece, step in zip(pieces[2:], (3, 5, 2, 6, 1, 7, 0)):
        piece[...] = chunk(step)


def add_kernel(first, piece, came, *refs):
    out = refs[-1]
    rows = slice(first, first + came.shape[1])
    if came.shape != piece.shape:
        out[...] = piece[...]
    out[:, rows] = (piece[:, rows].astype(jnp.float32) + came[...].astype(jnp.float32)).astype(jnp.bfloat16)


def add(piece, came, first=0, after=()):
    return kernel_call(
        functools.partial(add_kernel, first),
        jax.ShapeDtypeStruct(piece.shape, jnp.bfloat16),
        [VMEM_SPEC] * 2 + [pl.BlockSpec(memory_space=pl.ANY)] * len(after),
        name="ring_add",
    )(piece, came, *after)


def product_kernel(at, features, along_1, along_2, along_3, parts, keep, send, across, total):
    y, k = at[1], at[2]
    total[...] = jnp.zeros_like(total)
    for step, nodes in enumerate((features, along_1, along_2, along_3)):
        total[...] += lax.dot_general(
            nodes[...], parts[lax.rem(y + step, 4)], (((0,), (0,)), ((), ())), preferred_element_type=jnp.float32
        )
    keep[...] = total[pl.ds(pl.multiple_of(256 * k, 256), 256), :]
    send[...] = total[pl.ds(pl.multiple_of(256 * (1 - k), 256), 256), :].astype(jnp.bfloat16)
    for index in range(2):
        across[index] = parts[2 * index + 1 - lax.rem(y, 2)]


def half_kernel(keep, came, out):
    out[...] = (keep[...] + came[...].astype(jnp.float32)).astype(jnp.bfloat16).reshape(out.shape)


def sum_kernel(parts, out):
    total = parts[0].astype(jnp.float32)
    for index in range(1, parts.shape[0]):
        total = total + parts[index].astype(jnp.float32)
    total = total.astype(out.dtype)
    for index in range(out.shape[0]):
        out[index] = total


def share_kernel(at, half, parts, came, out, keep, send):
    sum_kernel(half, out)
    odd, high = lax.rem(at[1], 2), at[1] // 2

    def pair(index):
        return parts[2 * index + odd].astype(jnp.float32) + came[index].astype(jnp.float32)

    keep[...] = pair(high)
    send[...] = pair(1 - high).astype(jnp.bfloat16)


def total_kernel(share, keep, came, weight, out, grad_in):
    sum_kernel(share, out)
    agg = (keep[...] + came[...].astype(jnp.float32)).astype(jnp.bfloat16)
    grad_in[...] = lax.dot_general(
        agg, weight[...], (((1,), (1,)), ((), ())), preferred_element_type=jnp.float32
    ).astype(jnp.bfloat16)


def last_kernel(at, own, other, out):
    k = at[2]
    out[pl.ds(pl.multiple_of(256 * k, 256), 256), :] = own[...].reshape(256, WIDTH).astype(jnp.float32)
    out[pl.ds(pl.multiple_of(256 * (1 - k), 256), 256), :] = other[...].reshape(256, WIDTH).astype(jnp.float32)


def body(grad_out, relu_mask, features, weight, tile_vals, tile_rows, tile_cols, tile_count):
    x, h, k = (lax.axis_index(name) for name in ("x", "h", "k"))
    slope = (grad_out.astype(jnp.float32) * relu_mask.astype(jnp.float32)).astype(jnp.bfloat16)

    slope_h = permute(slope, h_swap)
    own = jnp.stack([slope] + [permute(slope, x_from(step)) for step in (1, 2, 3)])
    other = permute(own, k_swap)
    own_h = jnp.stack([slope_h] + [permute(slope_h, x_from(step)) for step in (1, 2, 3)])
    other_h = permute(own_h, k_swap)
    cols = tile_cols[0, 0]
    places = (cols // 4 - x) % 4 + 4 * ((cols // 2 % 2) ^ h) + 8 * ((cols % 2) ^ k)

    live = jnp.arange(SLOTS, dtype=jnp.int32) < tile_count[0, 0]
    codes = jnp.concatenate([jnp.where(live, tile_rows[0, 0], 32) * 16 + places, tile_count[0]])
    at = jnp.stack([lax.axis_index("z"), lax.axis_index("y"), k])
    piece = jax.ShapeDtypeStruct((4, 128, WIDTH), jnp.bfloat16)
    first = [
        jax.ShapeDtypeStruct((4, HALF, WIDTH), jnp.bfloat16),
        jax.ShapeDtypeStruct((4, 128 - HALF, WIDTH), jnp.bfloat16),
    ]
    pieces = kernel_call(
        block_kernel,
        first + [piece] * 7,
        [SMEM_SPEC] * 2 + [pl.BlockSpec(memory_space=pl.ANY)] + [VMEM_SPEC] * 4,
        [
            pltpu.VMEM((33, 128, WIDTH), jnp.float32),
            pltpu.VMEM((16, 128, WIDTH), jnp.bfloat16),
            pltpu.VMEM((SLOTS, 128, 128), jnp.bfloat16),
            pltpu.SemaphoreType.DMA,
        ],
        name="block_terms",
        limit=VMEM_WHOLE,
    )(at, codes, tile_vals[0, 0], own, own_h, other, other_h)

    along = [permute(features, y_from(step)) for step in (1, 2, 3)]
    up, down = pieces[0], pieces[1]
    for step in range(4):
        up, down = permute(up, z_up), permute(down, z_down)
        after = along[step - 1:step] if step else []
        if step == 0:
            up, down = add(pieces[2], up), add(pieces[3], down, HALF)
        elif step < 3:
            up, down = add(pieces[2 + 2 * step], up, 0, after), add(pieces[3 + 2 * step], down)
    parts = (
        pieces[8].astype(jnp.float32) + up.astype(jnp.float32) + down.astype(jnp.float32)
    ).astype(jnp.bfloat16)

    keep, send, across = kernel_call(
        product_kernel,
        (
            jax.ShapeDtypeStruct((256, WIDTH), jnp.float32),
            jax.ShapeDtypeStruct((256, WIDTH), jnp.bfloat16),
            jax.ShapeDtypeStruct((2, 128, WIDTH), jnp.bfloat16),
        ),
        [SMEM_SPEC] + [VMEM_SPEC] * 5,
        [pltpu.VMEM((WIDTH, WIDTH), jnp.float32)],
        name="weight_product",
    )(at, features, *along, parts)
    half = kernel_call(
        half_kernel, jax.ShapeDtypeStruct((32, 8, WIDTH), jnp.bfloat16), [VMEM_SPEC] * 2, name="weight_half"
    )(keep, permute(send, k_swap))
    half = lax.all_to_all(half, ("z", "x"), 0, 0, tiled=True)
    share, keep, send = kernel_call(
        share_kernel,
        (
            jax.ShapeDtypeStruct((8, 8, WIDTH), jnp.bfloat16),
            jax.ShapeDtypeStruct((128, WIDTH), jnp.float32),
            jax.ShapeDtypeStruct((128, WIDTH), jnp.bfloat16),
        ),
        [SMEM_SPEC] + [VMEM_SPEC] * 3,
        name="weight_share",
    )(at, half, parts, permute(across, y_flip(1)))
    send = permute(send, y_flip(2))
    share = lax.all_to_all(share, ("y", "h"), 0, 0, tiled=True)
    half, grad_in = kernel_call(
        total_kernel,
        (jax.ShapeDtypeStruct((32, 8, WIDTH), jnp.bfloat16), jax.ShapeDtypeStruct((128, WIDTH), jnp.bfloat16)),
        [VMEM_SPEC] * 4,
        name="weight_total",
    )(share, keep, send, weight)
    half = lax.all_to_all(half, ("z", "x"), 0, 0, tiled=True)
    grad_weight = kernel_call(
        last_kernel,
        jax.ShapeDtypeStruct((WIDTH, WIDTH), jnp.float32),
        [SMEM_SPEC] + [VMEM_SPEC] * 2,
        name="weight_order",
    )(at, half, permute(half, k_swap))
    return (grad_in, grad_weight)


def solution(mesh):
    fine = Mesh(mesh.devices.reshape(SIZES), AXES)
    nodes = P(AXES, None)
    rows, cols = AXES[:2], AXES[2:]
    return jax.shard_map(
        body,
        mesh=fine,
        in_specs=(
            nodes,
            nodes,
            nodes,
            P(),
            P(rows, cols, None, None, None),
            P(rows, cols, None),
            P(rows, cols, None),
            P(rows, cols),
        ),
        out_specs=(nodes, P()),
        check_vma=False,
    )
```

time: 216 us -> 179 us (0.83)
  starting transfers between devices: 45 us -> 104 us
  waiting for transfers between devices: 87.4 us -> 30.4 us
  blocking collectives: 53.6 us -> 27.2 us
  between operations: 16.3 us -> 1.67 us
  Pallas kernels: 7.18 us -> 12.2 us
  local copies, waits for them, and re-layouts: 3.89 us -> 0.8 us
    reduce_scatter x1 -> x0, waiting for transfers between devices: 63.7 us -> none  [body(): parts = lax.psum_scatter(terms, 'z', scatter_dimension=0, tiled=True)]
    ppermute x9 -> x24, starting transfers between devices: 38.9 us -> 96.1 us  [permute(): return lax.ppermute(value, AXES, pairs)]
    all_to_all x3 -> x2, blocking collectives: 53.6 us -> 27.2 us  [the longest x1 16.7 us: body(): half = lax.all_to_all(half, ('z', 'x'), 0, 0, tiled=True)]
    ppermute x9 -> x24, waiting for transfers between devices: 18 us -> 27.9 us  [permute(): return lax.ppermute(value, AXES, pairs)]
    pallas_call x5 -> x12, Pallas kernels: 7.18 us -> 12.2 us  [the longest x1 6.3 us: body(): kernel_call(block_kernel, first + [piece] * 7, [SMEM_SPEC] * 2 + [pl.Bloc...]
    unnamed x14 -> x6, local copies, waits for them, and re-layouts: 3.84 us -> 0.8 us
    all_to_all x1, waiting for transfers between devices: 5.27 us -> 2.49 us  [body(): half = lax.all_to_all(half, ('z', 'x'), 0, 0, tiled=True)]
  transfers between devices with their start and end apart: 12 -> 25, of which waited for: 9 -> 12; matrix products, arithmetic and copies ran while one was open for 0% -> 1% of each run, Pallas kernels for 0% -> 0%
where the time goes in v2:
time: 179 us; the launch traced here: 178 us
  starting transfers between devices  104 us (58%)
  waiting for transfers between devices  30.4 us (17%)
  blocking collectives  27.2 us (15%)
  Pallas kernels  12.2 us (7%)
  other arithmetic  2.21 us (1%)
    ppermute x24, starting transfers between devices, permute(): return lax.ppermute(value, AXES, pairs)  96.1 us
    ppermute x24, waiting for transfers between devices, permute(): return lax.ppermute(value, AXES, pairs)  27.9 us
    all_to_all x1, blocking collectives, body(): half = lax.all_to_all(half, ('z', 'x'), 0, 0, tiled=True)  16.7 us
    all_to_all x1, blocking collectives, body(): share = lax.all_to_all(share, ('y', 'h'), 0, 0, tiled=True)  10.5 us
    all_to_all x1, starting transfers between devices, body(): half = lax.all_to_all(half, ('z', 'x'), 0, 0, tiled=True)  7.74 us
    pallas_call x1, Pallas kernels, body(): kernel_call(block_kernel, first + [piece] * 7, [SMEM_SPEC] * 2 + [pl.Bloc...  6.3 us
  transfers between devices with their start and end apart: 25, of which 12 were waited for; matrix products, arithmetic and copies ran while one was open for 1% of the time, Pallas kernels for 0%

profile of v2, /device:TPU:1, one launch (start us, length us, event | category | flops | bytes accessed | tf_op | source)
XLA Modules:
  0.0 178.4 jit_solution(4013158959027782230)
XLA Ops:
  1.7 8.3 %collective-permute-start.6 = (bf16[128,512]{1,0:T(8,128)(2,1)S(1)}, bf16[128,512]{1,0:T(8,128)(2,1)S(1)}, u32[]{:S(2)}, u32[]{:S(2)}) collective-permute-start(bf16[128,512]{1,0:T(8,128)(2,1)S(1)} %multiply_convert_fusion), channel_id=1, source_target_pairs={{0,2},{1,3},{2,0},{3,1},{4,6},{5,7},{6,4},{7,5},{8,10},{9,11},{10,... | collective-permute-start | bytes 393224 | tf_op jit(solution)/shard_map/ppermute | solution.py:28
  9.9 4.7 %collective-permute-start.4 = (bf16[128,512]{1,0:T(8,128)(2,1)S(1)}, bf16[128,512]{1,0:T(8,128)(2,1)S(1)}, u32[]{:S(2)}, u32[]{:S(2)}) collective-permute-start(bf16[128,512]{1,0:T(8,128)(2,1)S(1)} %multiply_convert_fusion), channel_id=1, source_target_pairs={{0,8},{1,9},{2,10},{3,11},{4,12},{5,13},{6,14},{7,15},{8,0},{9,1},... | collective-permute-start | bytes 393224 | tf_op jit(solution)/shard_map/ppermute | solution.py:28
  14.6 2.2 %collective-permute-start.5 = (bf16[128,512]{1,0:T(8,128)(2,1)S(1)}, bf16[128,512]{1,0:T(8,128)(2,1)S(1)}, u32[]{:S(2)}, u32[]{:S(2)}) collective-permute-start(bf16[128,512]{1,0:T(8,128)(2,1)S(1)} %multiply_convert_fusion), channel_id=1, source_target_pairs={{0,4},{1,5},{2,6},{3,7},{4,8},{5,9},{6,10},{7,11},{8,12},{9,13},{1... | collective-permute-start | bytes 393224 | tf_op jit(solution)/shard_map/ppermute | solution.py:28
  16.8 4.3 %collective-permute-start.3 = (bf16[128,512]{1,0:T(8,128)(2,1)S(1)}, bf16[128,512]{1,0:T(8,128)(2,1)S(1)}, u32[]{:S(2)}, u32[]{:S(2)}) collective-permute-start(bf16[128,512]{1,0:T(8,128)(2,1)S(1)} %multiply_convert_fusion), channel_id=1, source_target_pairs={{0,12},{1,13},{2,14},{3,15},{4,0},{5,1},{6,2},{7,3},{8,4},{9,5},{1... | collective-permute-start | bytes 393224 | tf_op jit(solution)/shard_map/ppermute | solution.py:28
  21.1 1.9 %collective-permute-start.7 = (bf16[128,512]{1,0:T(8,128)(2,1)S(1)}, bf16[128,512]{1,0:T(8,128)(2,1)S(1)}, u32[]{:S(2)}, u32[]{:S(2)}) collective-permute-start(bf16[128,512]{1,0:T(8,128)(2,1)S(1)} %collective-permute-done.6), channel_id=1, source_target_pairs={{0,12},{1,13},{2,14},{3,15},{4,0},{5,1},{6,2},{7,3},{8,4},{9,5},{1... | collective-permute-start | bytes 393224 | tf_op jit(solution)/shard_map/ppermute | solution.py:28
  23.0 2.8 %collective-permute-start.8 = (bf16[128,512]{1,0:T(8,128)(2,1)S(1)}, bf16[128,512]{1,0:T(8,128)(2,1)S(1)}, u32[]{:S(2)}, u32[]{:S(2)}) collective-permute-start(bf16[128,512]{1,0:T(8,128)(2,1)S(1)} %collective-permute-done.6), channel_id=1, source_target_pairs={{0,8},{1,9},{2,10},{3,11},{4,12},{5,13},{6,14},{7,15},{8,0},{9,1},... | collective-permute-start | bytes 393224 | tf_op jit(solution)/shard_map/ppermute | solution.py:28
  25.9 2.5 %collective-permute-start.9 = (bf16[128,512]{1,0:T(8,128)(2,1)S(1)}, bf16[128,512]{1,0:T(8,128)(2,1)S(1)}, u32[]{:S(2)}, u32[]{:S(2)}) collective-permute-start(bf16[128,512]{1,0:T(8,128)(2,1)S(1)} %collective-permute-done.6), channel_id=1, source_target_pairs={{0,4},{1,5},{2,6},{3,7},{4,8},{5,9},{6,10},{7,11},{8,12},{9,13},{1... | collective-permute-start | bytes 393224 | tf_op jit(solution)/shard_map/ppermute | solution.py:28
  28.5 4.3 %collective-permute-start.10 = (bf16[4,128,512]{2,1,0:T(8,128)(2,1)S(1)}, bf16[4,128,512]{2,1,0:T(8,128)(2,1)S(1)}, u32[]{:S(2)}, u32[]{:S(2)}) collective-permute-start(bf16[4,128,512]{2,1,0:T(8,128)(2,1)S(1)} %pad_maximum_fusion.own), channel_id=1, source_target_pairs={{0,1},{1,0},{2,3},{3,2},{4,5},{5,4},{6,7},{7,6},{8,9},{9,8},{10,11... | collective-permute-start | bytes 1572872 | tf_op jit(solution)/shard_map/ppermute | solution.py:28
  34.0 4.3 %collective-permute-start.11 = (bf16[4,128,512]{2,1,0:T(8,128)(2,1)S(1)}, bf16[4,128,512]{2,1,0:T(8,128)(2,1)S(1)}, u32[]{:S(2)}, u32[]{:S(2)}) collective-permute-start(bf16[4,128,512]{2,1,0:T(8,128)(2,1)S(1)} %pad_maximum_fusion.1.own_h), channel_id=1, source_target_pairs={{0,1},{1,0},{2,3},{3,2},{4,5},{5,4},{6,7},{7,6},{8,9},{9,8},{10,11... | collective-permute-start | bytes 1572872 | tf_op jit(solution)/shard_map/ppermute | solution.py:28
  40.6 6.3 %block_terms.1 = (bf16[4,64,512]{2,1,0:T(8,128)(2,1)S(1)}, bf16[4,64,512]{2,1,0:T(8,128)(2,1)S(1)}, bf16[4,128,512]{2,1,0:T(8,128)(2,1)S(1)}, bf16[4,128,512]{2,...) custom-call(s32[3]{0:T(128)S(1)} %pad_add_fusion.at, ...), custom_call_target="tpu_custom_call" | custom-call | tf_op jit(solution)/shard_map/block_terms/pallas_call | solution.py:199
  46.9 3.0 %collective-permute-start.12 = (bf16[4,64,512]{2,1,0:T(8,128)(2,1)S(1)}, bf16[4,64,512]{2,1,0:T(8,128)(2,1)S(1)}, u32[]{:S(2)}, u32[]{:S(2)}) collective-permute-start(bf16[4,64,512]{2,1,0:T(8,128)(2,1)S(1)} %get-tuple-element.23), channel_id=1, source_target_pairs={{0,64},{1,65},{2,66},{3,67},{4,68},{5,69},{6,70},{7,71},{8,72},{9,... | collective-permute-start | bytes 786440 | tf_op jit(solution)/shard_map/ppermute | solution.py:28
  50.0 7.6 %collective-permute-start.16 = (bf16[4,64,512]{2,1,0:T(8,128)(2,1)S(1)}, bf16[4,64,512]{2,1,0:T(8,128)(2,1)S(1)}, u32[]{:S(2)}, u32[]{:S(2)}) collective-permute-start(bf16[4,64,512]{2,1,0:T(8,128)(2,1)S(1)} %get-tuple-element.27), channel_id=1, source_target_pairs={{0,448},{1,449},{2,450},{3,451},{4,452},{5,453},{6,454},{7,455},{8... | collective-permute-start | bytes 786440 | tf_op jit(solution)/shard_map/ppermute | solution.py:28
  57.6 4.4 %collective-permute-done.12.came = bf16[4,64,512]{2,1,0:T(8,128)(2,1)S(1)} collective-permute-done((bf16[4,64,512]{2,1,0:T(8,128)(2,1)S(1)}, bf16[4,64,512]{2,1,0:T(8,128)(2,1)S(1)}, u32[]{:S(2)}, u32[]{:S(2)}) %collective-permute-start.12) | collective-permute-done | bytes 262176 | tf_op jit(solution)/shard_map/ppermute | solution.py:28
  62.1 1.9 %collective-permute-start.13 = (bf16[4,128,512]{2,1,0:T(8,128)(2,1)S(1)}, bf16[4,128,512]{2,1,0:T(8,128)(2,1)S(1)}, u32[]{:S(2)}, u32[]{:S(2)}) collective-permute-start(bf16[4,128,512]{2,1,0:T(8,128)(2,1)S(1)} %ring_add.6), channel_id=1, source_target_pairs={{0,64},{1,65},{2,66},{3,67},{4,68},{5,69},{6,70},{7,71},{8,72},{9,... | collective-permute-start | bytes 1572872 | tf_op jit(solution)/shard_map/ppermute | solution.py:28
  64.1 4.6 %collective-permute-start.17 = (bf16[4,128,512]{2,1,0:T(8,128)(2,1)S(1)}, bf16[4,128,512]{2,1,0:T(8,128)(2,1)S(1)}, u32[]{:S(2)}, u32[]{:S(2)}) collective-permute-start(bf16[4,128,512]{2,1,0:T(8,128)(2,1)S(1)} %ring_add.9), channel_id=1, source_target_pairs={{0,448},{1,449},{2,450},{3,451},{4,452},{5,453},{6,454},{7,455},{8... | collective-permute-start | bytes 1572872 | tf_op jit(solution)/shard_map/ppermute | solution.py:28
  68.7 3.6 %collective-permute-start = (bf16[128,512]{1,0:T(8,128)(2,1)S(1)}, bf16[128,512]{1,0:T(8,128)(2,1)S(1)}, u32[]{:S(2)}, u32[]{:S(2)}) collective-permute-start(bf16[128,512]{1,0:T(8,128)(2,1)S(1)} %copy-done.1), channel_id=1, source_target_pairs={{0,48},{1,49},{2,50},{3,51},{4,52},{5,53},{6,54},{7,55},{8,56},{9,... | collective-permute-start | bytes 393224 | tf_op jit(solution)/shard_map/ppermute | solution.py:28
  72.3 3.9 %collective-permute-done.refs_0_.along_1 = bf16[128,512]{1,0:T(8,128)(2,1)S(1)} collective-permute-done((bf16[128,512]{1,0:T(8,128)(2,1)S(1)}, bf16[128,512]{1,0:T(8,128)(2,1)S(1)}, u32[]{:S(2)}, u32[]{:S(2)}) %collective-permute-start) | collective-permute-done | bytes 131104 | tf_op jit(solution)/shard_map/ppermute | solution.py:28
  77.9 1.9 %collective-permute-start.14 = (bf16[4,128,512]{2,1,0:T(8,128)(2,1)S(1)}, bf16[4,128,512]{2,1,0:T(8,128)(2,1)S(1)}, u32[]{:S(2)}, u32[]{:S(2)}) collective-permute-start(bf16[4,128,512]{2,1,0:T(8,128)(2,1)S(1)} %ring_add.7), channel_id=1, source_target_pairs={{0,64},{1,65},{2,66},{3,67},{4,68},{5,69},{6,70},{7,71},{8,72},{9,... | collective-permute-start | bytes 1572872 | tf_op jit(solution)/shard_map/ppermute | solution.py:28
  80.0 4.6 %collective-permute-start.18 = (bf16[4,128,512]{2,1,0:T(8,128)(2,1)S(1)}, bf16[4,128,512]{2,1,0:T(8,128)(2,1)S(1)}, u32[]{:S(2)}, u32[]{:S(2)}) collective-permute-start(bf16[4,128,512]{2,1,0:T(8,128)(2,1)S(1)} %ring_add.10), channel_id=1, source_target_pairs={{0,448},{1,449},{2,450},{3,451},{4,452},{5,453},{6,454},{7,455},{8... | collective-permute-start | bytes 1572872 | tf_op jit(solution)/shard_map/ppermute | solution.py:28
  84.5 2.4 %collective-permute-start.1 = (bf16[128,512]{1,0:T(8,128)(2,1)S(1)}, bf16[128,512]{1,0:T(8,128)(2,1)S(1)}, u32[]{:S(2)}, u32[]{:S(2)}) collective-permute-start(bf16[128,512]{1,0:T(8,128)(2,1)S(1)} %copy-done.1), channel_id=1, source_target_pairs={{0,32},{1,33},{2,34},{3,35},{4,36},{5,37},{6,38},{7,39},{8,40},{9,... | collective-permute-start | bytes 393224 | tf_op jit(solution)/shard_map/ppermute | solution.py:28
  86.9 4.5 %collective-permute-done.1.refs_0_.along_2 = bf16[128,512]{1,0:T(8,128)(2,1)S(1)} collective-permute-done((bf16[128,512]{1,0:T(8,128)(2,1)S(1)}, bf16[128,512]{1,0:T(8,128)(2,1)S(1)}, u32[]{:S(2)}, u32[]{:S(2)}) %collective-permute-start.1) | collective-permute-done | bytes 131104 | tf_op jit(solution)/shard_map/ppermute | solution.py:28
  94.8 4.7 %collective-permute-start.19 = (bf16[4,128,512]{2,1,0:T(8,128)(2,1)S(1)}, bf16[4,128,512]{2,1,0:T(8,128)(2,1)S(1)}, u32[]{:S(2)}, u32[]{:S(2)}) collective-permute-start(bf16[4,128,512]{2,1,0:T(8,128)(2,1)S(1)} %ring_add.11), channel_id=1, source_target_pairs={{0,448},{1,449},{2,450},{3,451},{4,452},{5,453},{6,454},{7,455},{8... | collective-permute-start | bytes 1572872 | tf_op jit(solution)/shard_map/ppermute | solution.py:28
  99.5 5.4 %collective-permute-start.2 = (bf16[128,512]{1,0:T(8,128)(2,1)S(1)}, bf16[128,512]{1,0:T(8,128)(2,1)S(1)}, u32[]{:S(2)}, u32[]{:S(2)}) collective-permute-start(bf16[128,512]{1,0:T(8,128)(2,1)S(1)} %copy-done.1), channel_id=1, source_target_pairs={{0,16},{1,17},{2,18},{3,19},{4,20},{5,21},{6,22},{7,23},{8,24},{9,... | collective-permute-start | bytes 393224 | tf_op jit(solution)/shard_map/ppermute | solution.py:28
  108.4 8.3 %collective-permute-start.20 = (bf16[256,512]{1,0:T(8,128)(2,1)S(1)}, bf16[256,512]{1,0:T(8,128)(2,1)S(1)}, u32[]{:S(2)}, u32[]{:S(2)}) collective-permute-start(bf16[256,512]{1,0:T(8,128)(2,1)S(1)} %get-tuple-element.29), channel_id=1, source_target_pairs={{0,1},{1,0},{2,3},{3,2},{4,5},{5,4},{6,7},{7,6},{8,9},{9,8},{10,11... | collective-permute-start | bytes 786440 | tf_op jit(solution)/shard_map/ppermute | solution.py:28
  118.6 7.7 %all-to-all-start = ((bf16[32,8,512]{2,1,0:T(8,128)(2,1)}), bf16[32,8,512]{2,1,0:T(8,128)(2,1)S(1)}, u32[]{:S(2)}, u32[]{:S(2)}) async-start(bf16[32,8,512]{2,1,0:T(8,128)(2,1)} %weight_half.1), calls=%async_computation | async-start | bytes 524288 | tf_op jit(solution)/shard_map/all_to_all | solution.py:240
  126.4 2.0 %collective-permute-start.21 = (bf16[2,128,512]{2,1,0:T(8,128)(2,1)S(1)}, bf16[2,128,512]{2,1,0:T(8,128)(2,1)S(1)}, u32[]{:S(2)}, u32[]{:S(2)}) collective-permute-start(bf16[2,128,512]{2,1,0:T(8,128)(2,1)S(1)} %get-tuple-element.30), channel_id=1, source_target_pairs={{0,16},{1,17},{2,18},{3,19},{4,20},{5,21},{6,22},{7,23},{8,24},{9,... | collective-permute-start | bytes 786440 | tf_op jit(solution)/shard_map/ppermute | solution.py:28
  128.4 7.1 %collective-permute-done.21.came = bf16[2,128,512]{2,1,0:T(8,128)(2,1)S(1)} collective-permute-done((bf16[2,128,512]{2,1,0:T(8,128)(2,1)S(1)}, bf16[2,128,512]{2,1,0:T(8,128)(2,1)S(1)}, u32[]{:S(2)}, u32[]{:S(2)}) %collective-permute-start.21) | collective-permute-done | bytes 262176 | tf_op jit(solution)/shard_map/ppermute | solution.py:28
  135.4 2.5 %all-to-all-done.half = bf16[32,8,512]{2,1,0:T(8,128)(2,1)S(1)} async-done(((bf16[32,8,512]{2,1,0:T(8,128)(2,1)}), bf16[32,8,512]{2,1,0:T(8,128)(2,1)S(1)}, u32[]{:S(2)}, u32[]{:S(2)}) %all-to-all-start) | async-done | bytes 262176 | tf_op jit(solution)/shard_map/all_to_all | solution.py:240
  138.6 2.2 %collective-permute-start.22 = (bf16[128,512]{1,0:T(8,128)(2,1)S(1)}, bf16[128,512]{1,0:T(8,128)(2,1)S(1)}, u32[]{:S(2)}, u32[]{:S(2)}) collective-permute-start(bf16[128,512]{1,0:T(8,128)(2,1)S(1)} %get-tuple-element.33), channel_id=1, source_target_pairs={{0,32},{1,33},{2,34},{3,35},{4,36},{5,37},{6,38},{7,39},{8,40},{9,... | collective-permute-start | bytes 393224 | tf_op jit(solution)/shard_map/ppermute | solution.py:28
  140.8 10.5 %all_to_all.15.share = bf16[8,8,512]{2,1,0:T(8,128)(2,1)S(1)} all-to-all(bf16[8,8,512]{2,1,0:T(8,128)(2,1)S(1)} %get-tuple-element.31), channel_id=1, replica_groups=mesh['z'=8,'y'=4,'x'=4,'h'=2,'k'=2] {'y','h'}, dimensions={0} | all-to-all | bytes 131072 | tf_op jit(solution)/shard_map/all_to_all | solution.py:252
  152.3 16.7 %all_to_all.16.own = bf16[32,8,512]{2,1,0:T(8,128)(2,1)S(1)} all-to-all(bf16[32,8,512]{2,1,0:T(8,128)(2,1)S(1)} %get-tuple-element.35), channel_id=1, replica_groups=mesh['z'=8,'y'=4,'x'=4,'h'=2,'k'=2] {'z','x'}, dimensions={0} | all-to-all | bytes 524288 | tf_op jit(solution)/shard_map/all_to_all | solution.py:259
  169.0 6.6 %collective-permute-start.23 = (bf16[32,8,512]{2,1,0:T(8,128)(2,1)S(1)}, bf16[32,8,512]{2,1,0:T(8,128)(2,1)S(1)}, u32[]{:S(2)}, u32[]{:S(2)}) collective-permute-start(bf16[32,8,512]{2,1,0:T(8,128)(2,1)S(1)} %all_to_all.16.own), channel_id=1, source_target_pairs={{0,1},{1,0},{2,3},{3,2},{4,5},{5,4},{6,7},{7,6},{8,9},{9,8},{10,11... | collective-permute-start | bytes 786440 | tf_op jit(solution)/shard_map/ppermute | solution.py:28
  (45 shorter events, 18.9 us)
Async XLA Ops:
  1.7 19.5 %collective-permute-start.6 = (bf16[128,512]{1,0:T(8,128)(2,1)S(1)}, bf16[128,512]{1,0:T(8,128)(2,1)S(1)}, u32[]{:S(2)}, u32[]{:S(2)}) collective-permute-start(bf16[128,512]{1,0:T(8,128)(2,1)S(1)} %multiply_convert_fusion), channel_id=1, source_target_pairs={{0,2},{1,3},{2,0},{3,1},{4,6},{5,7},{6,4},{7,5},{8,10},{9,11},{10,... | collective-permute-start | bytes 393224 | tf_op jit(solution)/shard_map/ppermute | solution.py:28
  9.9 15.9 %collective-permute-start.4 = (bf16[128,512]{1,0:T(8,128)(2,1)S(1)}, bf16[128,512]{1,0:T(8,128)(2,1)S(1)}, u32[]{:S(2)}, u32[]{:S(2)}) collective-permute-start(bf16[128,512]{1,0:T(8,128)(2,1)S(1)} %multiply_convert_fusion), channel_id=1, source_target_pairs={{0,8},{1,9},{2,10},{3,11},{4,12},{5,13},{6,14},{7,15},{8,0},{9,1},... | collective-permute-start | bytes 393224 | tf_op jit(solution)/shard_map/ppermute | solution.py:28
  14.6 13.8 %collective-permute-start.5 = (bf16[128,512]{1,0:T(8,128)(2,1)S(1)}, bf16[128,512]{1,0:T(8,128)(2,1)S(1)}, u32[]{:S(2)}, u32[]{:S(2)}) collective-permute-start(bf16[128,512]{1,0:T(8,128)(2,1)S(1)} %multiply_convert_fusion), channel_id=1, source_target_pairs={{0,4},{1,5},{2,6},{3,7},{4,8},{5,9},{6,10},{7,11},{8,12},{9,13},{1... | collective-permute-start | bytes 393224 | tf_op jit(solution)/shard_map/ppermute | solution.py:28
  16.8 11.5 %collective-permute-start.3 = (bf16[128,512]{1,0:T(8,128)(2,1)S(1)}, bf16[128,512]{1,0:T(8,128)(2,1)S(1)}, u32[]{:S(2)}, u32[]{:S(2)}) collective-permute-start(bf16[128,512]{1,0:T(8,128)(2,1)S(1)} %multiply_convert_fusion), channel_id=1, source_target_pairs={{0,12},{1,13},{2,14},{3,15},{4,0},{5,1},{6,2},{7,3},{8,4},{9,5},{1... | collective-permute-start | bytes 393224 | tf_op jit(solution)/shard_map/ppermute | solution.py:28
  21.1 11.6 %collective-permute-start.7 = (bf16[128,512]{1,0:T(8,128)(2,1)S(1)}, bf16[128,512]{1,0:T(8,128)(2,1)S(1)}, u32[]{:S(2)}, u32[]{:S(2)}) collective-permute-start(bf16[128,512]{1,0:T(8,128)(2,1)S(1)} %collective-permute-done.6), channel_id=1, source_target_pairs={{0,12},{1,13},{2,14},{3,15},{4,0},{5,1},{6,2},{7,3},{8,4},{9,5},{1... | collective-permute-start | bytes 393224 | tf_op jit(solution)/shard_map/ppermute | solution.py:28
  23.0 9.7 %collective-permute-start.8 = (bf16[128,512]{1,0:T(8,128)(2,1)S(1)}, bf16[128,512]{1,0:T(8,128)(2,1)S(1)}, u32[]{:S(2)}, u32[]{:S(2)}) collective-permute-start(bf16[128,512]{1,0:T(8,128)(2,1)S(1)} %collective-permute-done.6), channel_id=1, source_target_pairs={{0,8},{1,9},{2,10},{3,11},{4,12},{5,13},{6,14},{7,15},{8,0},{9,1},... | collective-permute-start | bytes 393224 | tf_op jit(solution)/shard_map/ppermute | solution.py:28
  25.9 8.1 %collective-permute-start.9 = (bf16[128,512]{1,0:T(8,128)(2,1)S(1)}, bf16[128,512]{1,0:T(8,128)(2,1)S(1)}, u32[]{:S(2)}, u32[]{:S(2)}) collective-permute-start(bf16[128,512]{1,0:T(8,128)(2,1)S(1)} %collective-permute-done.6), channel_id=1, source_target_pairs={{0,4},{1,5},{2,6},{3,7},{4,8},{5,9},{6,10},{7,11},{8,12},{9,13},{1... | collective-permute-start | bytes 393224 | tf_op jit(solution)/shard_map/ppermute | solution.py:28
  28.5 11.3 %collective-permute-start.10 = (bf16[4,128,512]{2,1,0:T(8,128)(2,1)S(1)}, bf16[4,128,512]{2,1,0:T(8,128)(2,1)S(1)}, u32[]{:S(2)}, u32[]{:S(2)}) collective-permute-start(bf16[4,128,512]{2,1,0:T(8,128)(2,1)S(1)} %pad_maximum_fusion.own), channel_id=1, source_target_pairs={{0,1},{1,0},{2,3},{3,2},{4,5},{5,4},{6,7},{7,6},{8,9},{9,8},{10,11... | collective-permute-start | bytes 1572872 | tf_op jit(solution)/shard_map/ppermute | solution.py:28
  34.0 5.8 %collective-permute-start.11 = (bf16[4,128,512]{2,1,0:T(8,128)(2,1)S(1)}, bf16[4,128,512]{2,1,0:T(8,128)(2,1)S(1)}, u32[]{:S(2)}, u32[]{:S(2)}) collective-permute-start(bf16[4,128,512]{2,1,0:T(8,128)(2,1)S(1)} %pad_maximum_fusion.1.own_h), channel_id=1, source_target_pairs={{0,1},{1,0},{2,3},{3,2},{4,5},{5,4},{6,7},{7,6},{8,9},{9,8},{10,11... | collective-permute-start | bytes 1572872 | tf_op jit(solution)/shard_map/ppermute | solution.py:28
  39.8 0.8 copy-start.2
  40.6 28.1 %copy-start.1 = (bf16[128,512]{1,0:T(8,128)(2,1)S(1)}, bf16[128,512]{1,0:T(8,128)(2,1)}, u32[]{:S(2)}) copy-start(bf16[128,512]{1,0:T(8,128)(2,1)} %features.1) | copy-start | bytes 393220
  46.9 15.1 %collective-permute-start.12 = (bf16[4,64,512]{2,1,0:T(8,128)(2,1)S(1)}, bf16[4,64,512]{2,1,0:T(8,128)(2,1)S(1)}, u32[]{:S(2)}, u32[]{:S(2)}) collective-permute-start(bf16[4,64,512]{2,1,0:T(8,128)(2,1)S(1)} %get-tuple-element.23), channel_id=1, source_target_pairs={{0,64},{1,65},{2,66},{3,67},{4,68},{5,69},{6,70},{7,71},{8,72},{9,... | collective-permute-start | bytes 786440 | tf_op jit(solution)/shard_map/ppermute | solution.py:28
  50.0 14.1 %collective-permute-start.16 = (bf16[4,64,512]{2,1,0:T(8,128)(2,1)S(1)}, bf16[4,64,512]{2,1,0:T(8,128)(2,1)S(1)}, u32[]{:S(2)}, u32[]{:S(2)}) collective-permute-start(bf16[4,64,512]{2,1,0:T(8,128)(2,1)S(1)} %get-tuple-element.27), channel_id=1, source_target_pairs={{0,448},{1,449},{2,450},{3,451},{4,452},{5,453},{6,454},{7,455},{8... | collective-permute-start | bytes 786440 | tf_op jit(solution)/shard_map/ppermute | solution.py:28
  62.1 15.7 %collective-permute-start.13 = (bf16[4,128,512]{2,1,0:T(8,128)(2,1)S(1)}, bf16[4,128,512]{2,1,0:T(8,128)(2,1)S(1)}, u32[]{:S(2)}, u32[]{:S(2)}) collective-permute-start(bf16[4,128,512]{2,1,0:T(8,128)(2,1)S(1)} %ring_add.6), channel_id=1, source_target_pairs={{0,64},{1,65},{2,66},{3,67},{4,68},{5,69},{6,70},{7,71},{8,72},{9,... | collective-permute-start | bytes 1572872 | tf_op jit(solution)/shard_map/ppermute | solution.py:28
  64.1 15.7 %collective-permute-start.17 = (bf16[4,128,512]{2,1,0:T(8,128)(2,1)S(1)}, bf16[4,128,512]{2,1,0:T(8,128)(2,1)S(1)}, u32[]{:S(2)}, u32[]{:S(2)}) collective-permute-start(bf16[4,128,512]{2,1,0:T(8,128)(2,1)S(1)} %ring_add.9), channel_id=1, source_target_pairs={{0,448},{1,449},{2,450},{3,451},{4,452},{5,453},{6,454},{7,455},{8... | collective-permute-start | bytes 1572872 | tf_op jit(solution)/shard_map/ppermute | solution.py:28
  68.7 7.5 %collective-permute-start = (bf16[128,512]{1,0:T(8,128)(2,1)S(1)}, bf16[128,512]{1,0:T(8,128)(2,1)S(1)}, u32[]{:S(2)}, u32[]{:S(2)}) collective-permute-start(bf16[128,512]{1,0:T(8,128)(2,1)S(1)} %copy-done.1), channel_id=1, source_target_pairs={{0,48},{1,49},{2,50},{3,51},{4,52},{5,53},{6,54},{7,55},{8,56},{9,... | collective-permute-start | bytes 393224 | tf_op jit(solution)/shard_map/ppermute | solution.py:28
  77.9 14.7 %collective-permute-start.14 = (bf16[4,128,512]{2,1,0:T(8,128)(2,1)S(1)}, bf16[4,128,512]{2,1,0:T(8,128)(2,1)S(1)}, u32[]{:S(2)}, u32[]{:S(2)}) collective-permute-start(bf16[4,128,512]{2,1,0:T(8,128)(2,1)S(1)} %ring_add.7), channel_id=1, source_target_pairs={{0,64},{1,65},{2,66},{3,67},{4,68},{5,69},{6,70},{7,71},{8,72},{9,... | collective-permute-start | bytes 1572872 | tf_op jit(solution)/shard_map/ppermute | solution.py:28
  80.0 14.7 %collective-permute-start.18 = (bf16[4,128,512]{2,1,0:T(8,128)(2,1)S(1)}, bf16[4,128,512]{2,1,0:T(8,128)(2,1)S(1)}, u32[]{:S(2)}, u32[]{:S(2)}) collective-permute-start(bf16[4,128,512]{2,1,0:T(8,128)(2,1)S(1)} %ring_add.10), channel_id=1, source_target_pairs={{0,448},{1,449},{2,450},{3,451},{4,452},{5,453},{6,454},{7,455},{8... | collective-permute-start | bytes 1572872 | tf_op jit(solution)/shard_map/ppermute | solution.py:28
  84.5 6.9 %collective-permute-start.1 = (bf16[128,512]{1,0:T(8,128)(2,1)S(1)}, bf16[128,512]{1,0:T(8,128)(2,1)S(1)}, u32[]{:S(2)}, u32[]{:S(2)}) collective-permute-start(bf16[128,512]{1,0:T(8,128)(2,1)S(1)} %copy-done.1), channel_id=1, source_target_pairs={{0,32},{1,33},{2,34},{3,35},{4,36},{5,37},{6,38},{7,39},{8,40},{9,... | collective-permute-start | bytes 393224 | tf_op jit(solution)/shard_map/ppermute | solution.py:28
  92.7 12.2 %collective-permute-start.15 = (bf16[4,128,512]{2,1,0:T(8,128)(2,1)S(1)}, bf16[4,128,512]{2,1,0:T(8,128)(2,1)S(1)}, u32[]{:S(2)}, u32[]{:S(2)}) collective-permute-start(bf16[4,128,512]{2,1,0:T(8,128)(2,1)S(1)} %ring_add.8), channel_id=1, source_target_pairs={{0,64},{1,65},{2,66},{3,67},{4,68},{5,69},{6,70},{7,71},{8,72},{9,... | collective-permute-start | bytes 1572872 | tf_op jit(solution)/shard_map/ppermute | solution.py:28
  94.8 56.5 %copy-start = (bf16[512,512]{1,0:T(8,128)(2,1)S(1)}, bf16[512,512]{1,0:T(8,128)(2,1)}, u32[]{:S(2)}) copy-start(bf16[512,512]{1,0:T(8,128)(2,1)} %weight.1) | copy-start | bytes 1572868
  94.8 10.8 %collective-permute-start.19 = (bf16[4,128,512]{2,1,0:T(8,128)(2,1)S(1)}, bf16[4,128,512]{2,1,0:T(8,128)(2,1)S(1)}, u32[]{:S(2)}, u32[]{:S(2)}) collective-permute-start(bf16[4,128,512]{2,1,0:T(8,128)(2,1)S(1)} %ring_add.11), channel_id=1, source_target_pairs={{0,448},{1,449},{2,450},{3,451},{4,452},{5,453},{6,454},{7,455},{8... | collective-permute-start | bytes 1572872 | tf_op jit(solution)/shard_map/ppermute | solution.py:28
  99.5 7.5 %collective-permute-start.2 = (bf16[128,512]{1,0:T(8,128)(2,1)S(1)}, bf16[128,512]{1,0:T(8,128)(2,1)S(1)}, u32[]{:S(2)}, u32[]{:S(2)}) collective-permute-start(bf16[128,512]{1,0:T(8,128)(2,1)S(1)} %copy-done.1), channel_id=1, source_target_pairs={{0,16},{1,17},{2,18},{3,19},{4,20},{5,21},{6,22},{7,23},{8,24},{9,... | collective-permute-start | bytes 393224 | tf_op jit(solution)/shard_map/ppermute | solution.py:28
  108.4 9.5 %collective-permute-start.20 = (bf16[256,512]{1,0:T(8,128)(2,1)S(1)}, bf16[256,512]{1,0:T(8,128)(2,1)S(1)}, u32[]{:S(2)}, u32[]{:S(2)}) collective-permute-start(bf16[256,512]{1,0:T(8,128)(2,1)S(1)} %get-tuple-element.29), channel_id=1, source_target_pairs={{0,1},{1,0},{2,3},{3,2},{4,5},{5,4},{6,7},{7,6},{8,9},{9,8},{10,11... | collective-permute-start | bytes 786440 | tf_op jit(solution)/shard_map/ppermute | solution.py:28
  118.6 19.3 %all-to-all-start = ((bf16[32,8,512]{2,1,0:T(8,128)(2,1)}), bf16[32,8,512]{2,1,0:T(8,128)(2,1)S(1)}, u32[]{:S(2)}, u32[]{:S(2)}) async-start(bf16[32,8,512]{2,1,0:T(8,128)(2,1)} %weight_half.1), calls=%async_computation | async-start | bytes 524288 | tf_op jit(solution)/shard_map/all_to_all | solution.py:240
  126.4 9.1 %collective-permute-start.21 = (bf16[2,128,512]{2,1,0:T(8,128)(2,1)S(1)}, bf16[2,128,512]{2,1,0:T(8,128)(2,1)S(1)}, u32[]{:S(2)}, u32[]{:S(2)}) collective-permute-start(bf16[2,128,512]{2,1,0:T(8,128)(2,1)S(1)} %get-tuple-element.30), channel_id=1, source_target_pairs={{0,16},{1,17},{2,18},{3,19},{4,20},{5,21},{6,22},{7,23},{8,24},{9,... | collective-permute-start | bytes 786440 | tf_op jit(solution)/shard_map/ppermute | solution.py:28
  138.6 12.7 %collective-permute-start.22 = (bf16[128,512]{1,0:T(8,128)(2,1)S(1)}, bf16[128,512]{1,0:T(8,128)(2,1)S(1)}, u32[]{:S(2)}, u32[]{:S(2)}) collective-permute-start(bf16[128,512]{1,0:T(8,128)(2,1)S(1)} %get-tuple-element.33), channel_id=1, source_target_pairs={{0,32},{1,33},{2,34},{3,35},{4,36},{5,37},{6,38},{7,39},{8,40},{9,... | collective-permute-start | bytes 393224 | tf_op jit(solution)/shard_map/ppermute | solution.py:28
  169.0 7.8 %collective-permute-start.23 = (bf16[32,8,512]{2,1,0:T(8,128)(2,1)S(1)}, bf16[32,8,512]{2,1,0:T(8,128)(2,1)S(1)}, u32[]{:S(2)}, u32[]{:S(2)}) collective-permute-start(bf16[32,8,512]{2,1,0:T(8,128)(2,1)S(1)} %all_to_all.16.own), channel_id=1, source_target_pairs={{0,1},{1,0},{2,3},{3,2},{4,5},{5,4},{6,7},{7,6},{8,9},{9,8},{10,11... | collective-permute-start | bytes 786440 | tf_op jit(solution)/shard_map/ppermute | solution.py:28

commit v3 on v2

--- a/solution.py
+++ b/solution.py
@@ -41,6 +41,11 @@
         return (z, y, (x - step) % 4, h, k)
 
     return move
+
+
+def around(block):
+    far = permute(block, x_from(2))
+    return [block, permute(block, x_from(1)), far, permute(block, x_from(3))]
 
 
 def y_from(step):
@@ -78,13 +83,15 @@
 
 
 def block_kernel(at, codes, vals, own, own_h, other, other_h, *refs):
-    pieces, (acc, source, held, sem) = refs[:9], refs[9:]
-    copy = pltpu.make_async_copy(vals, held, sem)
-    copy.start()
+    pieces, (acc, source, held, sems) = refs[-13:-4], refs[-4:]
+    copies = [pltpu.make_async_copy(vals, held, sems.at[4])]
     for index, blocks in enumerate((own, own_h, other, other_h)):
-        source[4 * index:4 * index + 4] = blocks[...]
+        copies.append(pltpu.make_async_copy(blocks, source.at[pl.ds(4 * index, 4)], sems.at[index]))
+    for copy in copies:
+        copy.start()
     acc[...] = jnp.zeros_like(acc)
-    copy.wait()
+    for copy in copies:
+        copy.wait()
 
     def group(index, carry):
         terms = []
@@ -181,15 +188,15 @@
     slope = (grad_out.astype(jnp.float32) * relu_mask.astype(jnp.float32)).astype(jnp.bfloat16)
 
     slope_h = permute(slope, h_swap)
-    own = jnp.stack([slope] + [permute(slope, x_from(step)) for step in (1, 2, 3)])
+    own = jnp.stack(around(slope))
     other = permute(own, k_swap)
-    own_h = jnp.stack([slope_h] + [permute(slope_h, x_from(step)) for step in (1, 2, 3)])
+    own_h = jnp.stack(around(slope_h))
     other_h = permute(own_h, k_swap)
     cols = tile_cols[0, 0]
     places = (cols // 4 - x) % 4 + 4 * ((cols // 2 % 2) ^ h) + 8 * ((cols % 2) ^ k)
 
     live = jnp.arange(SLOTS, dtype=jnp.int32) < tile_count[0, 0]
-    codes = jnp.concatenate([jnp.where(live, tile_rows[0, 0], 32) * 16 + places, tile_count[0]])
+    codes = jnp.concatenate([jnp.where(live, tile_rows[0, 0] * 16 + places, 32 * 16), tile_count[0]])
     at = jnp.stack([lax.axis_index("z"), lax.axis_index("y"), k])
     piece = jax.ShapeDtypeStruct((4, 128, WIDTH), jnp.bfloat16)
     first = [
@@ -199,12 +206,12 @@
     pieces = kernel_call(
         block_kernel,
         first + [piece] * 7,
-        [SMEM_SPEC] * 2 + [pl.BlockSpec(memory_space=pl.ANY)] + [VMEM_SPEC] * 4,
+        [SMEM_SPEC] * 2 + [pl.BlockSpec(memory_space=pl.ANY)] * 5,
         [
             pltpu.VMEM((33, 128, WIDTH), jnp.float32),
             pltpu.VMEM((16, 128, WIDTH), jnp.bfloat16),
             pltpu.VMEM((SLOTS, 128, 128), jnp.bfloat16),
-            pltpu.SemaphoreType.DMA,
+            pltpu.SemaphoreType.DMA((5,)),
         ],
         name="block_terms",
         limit=VMEM_WHOLE,
@@ -218,7 +225,7 @@
         if step == 0:
             up, down = add(pieces[2], up), add(pieces[3], down, HALF)
         elif step < 3:
-            up, down = add(pieces[2 + 2 * step], up, 0, after), add(pieces[3 + 2 * step], down)
+            up, down = add(pieces[2 + 2 * step], up), add(pieces[3 + 2 * step], down, 0, after)
     parts = (
         pieces[8].astype(jnp.float32) + up.astype(jnp.float32) + down.astype(jnp.float32)
     ).astype(jnp.bfloat16)

time: 179 us -> 179 us (level)
  starting transfers between devices: 104 us -> 115 us
  waiting for transfers between devices: 30.4 us -> 22.4 us
  Pallas kernels: 12.2 us -> 9.87 us
    ppermute x24, starting transfers between devices: 96.1 us -> 105 us  [permute(): return lax.ppermute(value, AXES, pairs)]
    ppermute x24, waiting for transfers between devices: 27.9 us -> 19.9 us  [permute(): return lax.ppermute(value, AXES, pairs)]
    all_to_all x1, starting transfers between devices: 7.74 us -> 10.3 us  [body(): half = lax.all_to_all(half, ('z', 'x'), 0, 0, tiled=True)]
    pallas_call x1, Pallas kernels: 6.3 us -> 3.96 us  [body(): kernel_call(block_kernel, first + [piece] * 7, [SMEM_SPEC] * 2 + [pl.Bloc...]
  transfers between devices with their start and end apart: 25 -> 25, of which waited for: 12 -> 9; matrix products, arithmetic and copies ran while one was open for 1% -> 1% of each run, Pallas kernels for 0% -> 0%
where the time goes in v3:
time: 179 us; the launch traced here: 178 us
  starting transfers between devices  115 us (64%)
  blocking collectives  25.7 us (14%)
  waiting for transfers between devices  22.4 us (13%)
  Pallas kernels  9.87 us (6%)
  other arithmetic  2.22 us (1%)
    ppermute x24, starting transfers between devices, permute(): return lax.ppermute(value, AXES, pairs)  105 us
    ppermute x24, waiting for transfers between devices, permute(): return lax.ppermute(value, AXES, pairs)  19.9 us
    all_to_all x1, blocking collectives, body(): half = lax.all_to_all(half, ('z', 'x'), 0, 0, tiled=True)  16.7 us
    all_to_all x1, starting transfers between devices, body(): half = lax.all_to_all(half, ('z', 'x'), 0, 0, tiled=True)  10.3 us
    all_to_all x1, blocking collectives, body(): share = lax.all_to_all(share, ('y', 'h'), 0, 0, tiled=True)  9.02 us
    pallas_call x1, Pallas kernels, body(): kernel_call(block_kernel, first + [piece] * 7, [SMEM_SPEC] * 2 + [pl.Bloc...  3.96 us
  transfers between devices with their start and end apart: 25, of which 9 were waited for; matrix products, arithmetic and copies ran while one was open for 1% of the time, Pallas kernels for 0%

profile of v3, /device:TPU:1, one launch (start us, length us, event | category | flops | bytes accessed | tf_op | source)
XLA Modules:
  0.0 177.7 jit_solution(13691738861490220668)
XLA Ops:
  1.7 8.3 %collective-permute-start.6 = (bf16[128,512]{1,0:T(8,128)(2,1)S(1)}, bf16[128,512]{1,0:T(8,128)(2,1)S(1)}, u32[]{:S(2)}, u32[]{:S(2)}) collective-permute-start(bf16[128,512]{1,0:T(8,128)(2,1)S(1)} %multiply_convert_fusion), channel_id=1, source_target_pairs={{0,2},{1,3},{2,0},{3,1},{4,6},{5,7},{6,4},{7,5},{8,10},{9,11},{10,... | collective-permute-start | bytes 393224 | tf_op jit(solution)/shard_map/ppermute | solution.py:28
  9.9 4.7 %collective-permute-start.4 = (bf16[128,512]{1,0:T(8,128)(2,1)S(1)}, bf16[128,512]{1,0:T(8,128)(2,1)S(1)}, u32[]{:S(2)}, u32[]{:S(2)}) collective-permute-start(bf16[128,512]{1,0:T(8,128)(2,1)S(1)} %multiply_convert_fusion), channel_id=1, source_target_pairs={{0,8},{1,9},{2,10},{3,11},{4,12},{5,13},{6,14},{7,15},{8,0},{9,1},... | collective-permute-start | bytes 393224 | tf_op jit(solution)/shard_map/ppermute | solution.py:28
  14.6 2.2 %collective-permute-start.5 = (bf16[128,512]{1,0:T(8,128)(2,1)S(1)}, bf16[128,512]{1,0:T(8,128)(2,1)S(1)}, u32[]{:S(2)}, u32[]{:S(2)}) collective-permute-start(bf16[128,512]{1,0:T(8,128)(2,1)S(1)} %multiply_convert_fusion), channel_id=1, source_target_pairs={{0,4},{1,5},{2,6},{3,7},{4,8},{5,9},{6,10},{7,11},{8,12},{9,13},{1... | collective-permute-start | bytes 393224 | tf_op jit(solution)/shard_map/ppermute | solution.py:28
  16.8 4.3 %collective-permute-start.3 = (bf16[128,512]{1,0:T(8,128)(2,1)S(1)}, bf16[128,512]{1,0:T(8,128)(2,1)S(1)}, u32[]{:S(2)}, u32[]{:S(2)}) collective-permute-start(bf16[128,512]{1,0:T(8,128)(2,1)S(1)} %multiply_convert_fusion), channel_id=1, source_target_pairs={{0,12},{1,13},{2,14},{3,15},{4,0},{5,1},{6,2},{7,3},{8,4},{9,5},{1... | collective-permute-start | bytes 393224 | tf_op jit(solution)/shard_map/ppermute | solution.py:28
  21.1 1.9 %collective-permute-start.7 = (bf16[128,512]{1,0:T(8,128)(2,1)S(1)}, bf16[128,512]{1,0:T(8,128)(2,1)S(1)}, u32[]{:S(2)}, u32[]{:S(2)}) collective-permute-start(bf16[128,512]{1,0:T(8,128)(2,1)S(1)} %collective-permute-done.6), channel_id=1, source_target_pairs={{0,12},{1,13},{2,14},{3,15},{4,0},{5,1},{6,2},{7,3},{8,4},{9,5},{1... | collective-permute-start | bytes 393224 | tf_op jit(solution)/shard_map/ppermute | solution.py:28
  23.0 2.8 %collective-permute-start.8 = (bf16[128,512]{1,0:T(8,128)(2,1)S(1)}, bf16[128,512]{1,0:T(8,128)(2,1)S(1)}, u32[]{:S(2)}, u32[]{:S(2)}) collective-permute-start(bf16[128,512]{1,0:T(8,128)(2,1)S(1)} %collective-permute-done.6), channel_id=1, source_target_pairs={{0,8},{1,9},{2,10},{3,11},{4,12},{5,13},{6,14},{7,15},{8,0},{9,1},... | collective-permute-start | bytes 393224 | tf_op jit(solution)/shard_map/ppermute | solution.py:28
  25.9 2.5 %collective-permute-start.9 = (bf16[128,512]{1,0:T(8,128)(2,1)S(1)}, bf16[128,512]{1,0:T(8,128)(2,1)S(1)}, u32[]{:S(2)}, u32[]{:S(2)}) collective-permute-start(bf16[128,512]{1,0:T(8,128)(2,1)S(1)} %collective-permute-done.6), channel_id=1, source_target_pairs={{0,4},{1,5},{2,6},{3,7},{4,8},{5,9},{6,10},{7,11},{8,12},{9,13},{1... | collective-permute-start | bytes 393224 | tf_op jit(solution)/shard_map/ppermute | solution.py:28
  28.5 4.3 %collective-permute-start.10 = (bf16[4,128,512]{2,1,0:T(8,128)(2,1)S(1)}, bf16[4,128,512]{2,1,0:T(8,128)(2,1)S(1)}, u32[]{:S(2)}, u32[]{:S(2)}) collective-permute-start(bf16[4,128,512]{2,1,0:T(8,128)(2,1)S(1)} %pad_maximum_fusion.own), channel_id=1, source_target_pairs={{0,1},{1,0},{2,3},{3,2},{4,5},{5,4},{6,7},{7,6},{8,9},{9,8},{10,11... | collective-permute-start | bytes 1572872 | tf_op jit(solution)/shard_map/ppermute | solution.py:28
  34.0 4.3 %collective-permute-start.11 = (bf16[4,128,512]{2,1,0:T(8,128)(2,1)S(1)}, bf16[4,128,512]{2,1,0:T(8,128)(2,1)S(1)}, u32[]{:S(2)}, u32[]{:S(2)}) collective-permute-start(bf16[4,128,512]{2,1,0:T(8,128)(2,1)S(1)} %pad_maximum_fusion.1.own_h), channel_id=1, source_target_pairs={{0,1},{1,0},{2,3},{3,2},{4,5},{5,4},{6,7},{7,6},{8,9},{9,8},{10,11... | collective-permute-start | bytes 1572872 | tf_op jit(solution)/shard_map/ppermute | solution.py:28
  40.6 4.0 %block_terms.1 = (bf16[4,64,512]{2,1,0:T(8,128)(2,1)S(1)}, bf16[4,64,512]{2,1,0:T(8,128)(2,1)S(1)}, bf16[4,128,512]{2,1,0:T(8,128)(2,1)S(1)}, bf16[4,128,512]{2,...) custom-call(s32[3]{0:T(128)S(1)} %pad_add_fusion.at, ...), custom_call_target="tpu_custom_call" | custom-call | tf_op jit(solution)/shard_map/block_terms/pallas_call | solution.py:206
  44.6 4.0 %collective-permute-start.12 = (bf16[4,64,512]{2,1,0:T(8,128)(2,1)S(1)}, bf16[4,64,512]{2,1,0:T(8,128)(2,1)S(1)}, u32[]{:S(2)}, u32[]{:S(2)}) collective-permute-start(bf16[4,64,512]{2,1,0:T(8,128)(2,1)S(1)} %get-tuple-element.23), channel_id=1, source_target_pairs={{0,64},{1,65},{2,66},{3,67},{4,68},{5,69},{6,70},{7,71},{8,72},{9,... | collective-permute-start | bytes 786440 | tf_op jit(solution)/shard_map/ppermute | solution.py:28
  48.6 8.6 %collective-permute-start.16 = (bf16[4,64,512]{2,1,0:T(8,128)(2,1)S(1)}, bf16[4,64,512]{2,1,0:T(8,128)(2,1)S(1)}, u32[]{:S(2)}, u32[]{:S(2)}) collective-permute-start(bf16[4,64,512]{2,1,0:T(8,128)(2,1)S(1)} %get-tuple-element.27), channel_id=1, source_target_pairs={{0,448},{1,449},{2,450},{3,451},{4,452},{5,453},{6,454},{7,455},{8... | collective-permute-start | bytes 786440 | tf_op jit(solution)/shard_map/ppermute | solution.py:28
  57.2 3.3 %collective-permute-done.12.came = bf16[4,64,512]{2,1,0:T(8,128)(2,1)S(1)} collective-permute-done((bf16[4,64,512]{2,1,0:T(8,128)(2,1)S(1)}, bf16[4,64,512]{2,1,0:T(8,128)(2,1)S(1)}, u32[]{:S(2)}, u32[]{:S(2)}) %collective-permute-start.12) | collective-permute-done | bytes 262176 | tf_op jit(solution)/shard_map/ppermute | solution.py:28
  60.6 1.9 %collective-permute-start.13 = (bf16[4,128,512]{2,1,0:T(8,128)(2,1)S(1)}, bf16[4,128,512]{2,1,0:T(8,128)(2,1)S(1)}, u32[]{:S(2)}, u32[]{:S(2)}) collective-permute-start(bf16[4,128,512]{2,1,0:T(8,128)(2,1)S(1)} %ring_add.6), channel_id=1, source_target_pairs={{0,64},{1,65},{2,66},{3,67},{4,68},{5,69},{6,70},{7,71},{8,72},{9,... | collective-permute-start | bytes 1572872 | tf_op jit(solution)/shard_map/ppermute | solution.py:28
  62.6 4.6 %collective-permute-start.17 = (bf16[4,128,512]{2,1,0:T(8,128)(2,1)S(1)}, bf16[4,128,512]{2,1,0:T(8,128)(2,1)S(1)}, u32[]{:S(2)}, u32[]{:S(2)}) collective-permute-start(bf16[4,128,512]{2,1,0:T(8,128)(2,1)S(1)} %ring_add.9), channel_id=1, source_target_pairs={{0,448},{1,449},{2,450},{3,451},{4,452},{5,453},{6,454},{7,455},{8... | collective-permute-start | bytes 1572872 | tf_op jit(solution)/shard_map/ppermute | solution.py:28
  67.2 3.6 %collective-permute-start = (bf16[128,512]{1,0:T(8,128)(2,1)S(1)}, bf16[128,512]{1,0:T(8,128)(2,1)S(1)}, u32[]{:S(2)}, u32[]{:S(2)}) collective-permute-start(bf16[128,512]{1,0:T(8,128)(2,1)S(1)} %copy-done.1), channel_id=1, source_target_pairs={{0,48},{1,49},{2,50},{3,51},{4,52},{5,53},{6,54},{7,55},{8,56},{9,... | collective-permute-start | bytes 393224 | tf_op jit(solution)/shard_map/ppermute | solution.py:28
  70.9 4.3 %collective-permute-done.13.came = bf16[4,128,512]{2,1,0:T(8,128)(2,1)S(1)} collective-permute-done((bf16[4,128,512]{2,1,0:T(8,128)(2,1)S(1)}, bf16[4,128,512]{2,1,0:T(8,128)(2,1)S(1)}, u32[]{:S(2)}, u32[]{:S(2)}) %collective-permute-start.13) | collective-permute-done | bytes 524320 | tf_op jit(solution)/shard_map/ppermute | solution.py:28
  75.2 1.9 %collective-permute-start.14 = (bf16[4,128,512]{2,1,0:T(8,128)(2,1)S(1)}, bf16[4,128,512]{2,1,0:T(8,128)(2,1)S(1)}, u32[]{:S(2)}, u32[]{:S(2)}) collective-permute-start(bf16[4,128,512]{2,1,0:T(8,128)(2,1)S(1)} %ring_add.7), channel_id=1, source_target_pairs={{0,64},{1,65},{2,66},{3,67},{4,68},{5,69},{6,70},{7,71},{8,72},{9,... | collective-permute-start | bytes 1572872 | tf_op jit(solution)/shard_map/ppermute | solution.py:28
  77.3 4.6 %collective-permute-start.18 = (bf16[4,128,512]{2,1,0:T(8,128)(2,1)S(1)}, bf16[4,128,512]{2,1,0:T(8,128)(2,1)S(1)}, u32[]{:S(2)}, u32[]{:S(2)}) collective-permute-start(bf16[4,128,512]{2,1,0:T(8,128)(2,1)S(1)} %ring_add.10), channel_id=1, source_target_pairs={{0,448},{1,449},{2,450},{3,451},{4,452},{5,453},{6,454},{7,455},{8... | collective-permute-start | bytes 1572872 | tf_op jit(solution)/shard_map/ppermute | solution.py:28
  81.9 6.2 %collective-permute-start.1 = (bf16[128,512]{1,0:T(8,128)(2,1)S(1)}, bf16[128,512]{1,0:T(8,128)(2,1)S(1)}, u32[]{:S(2)}, u32[]{:S(2)}) collective-permute-start(bf16[128,512]{1,0:T(8,128)(2,1)S(1)} %copy-done.1), channel_id=1, source_target_pairs={{0,32},{1,33},{2,34},{3,35},{4,36},{5,37},{6,38},{7,39},{8,40},{9,... | collective-permute-start | bytes 393224 | tf_op jit(solution)/shard_map/ppermute | solution.py:28
  89.0 1.9 %collective-permute-start.15 = (bf16[4,128,512]{2,1,0:T(8,128)(2,1)S(1)}, bf16[4,128,512]{2,1,0:T(8,128)(2,1)S(1)}, u32[]{:S(2)}, u32[]{:S(2)}) collective-permute-start(bf16[4,128,512]{2,1,0:T(8,128)(2,1)S(1)} %ring_add.8), channel_id=1, source_target_pairs={{0,64},{1,65},{2,66},{3,67},{4,68},{5,69},{6,70},{7,71},{8,72},{9,... | collective-permute-start | bytes 1572872 | tf_op jit(solution)/shard_map/ppermute | solution.py:28
  91.1 4.7 %collective-permute-start.19 = (bf16[4,128,512]{2,1,0:T(8,128)(2,1)S(1)}, bf16[4,128,512]{2,1,0:T(8,128)(2,1)S(1)}, u32[]{:S(2)}, u32[]{:S(2)}) collective-permute-start(bf16[4,128,512]{2,1,0:T(8,128)(2,1)S(1)} %ring_add.11), channel_id=1, source_target_pairs={{0,448},{1,449},{2,450},{3,451},{4,452},{5,453},{6,454},{7,455},{8... | collective-permute-start | bytes 1572872 | tf_op jit(solution)/shard_map/ppermute | solution.py:28
  95.8 7.8 %collective-permute-start.2 = (bf16[128,512]{1,0:T(8,128)(2,1)S(1)}, bf16[128,512]{1,0:T(8,128)(2,1)S(1)}, u32[]{:S(2)}, u32[]{:S(2)}) collective-permute-start(bf16[128,512]{1,0:T(8,128)(2,1)S(1)} %copy-done.1), channel_id=1, source_target_pairs={{0,16},{1,17},{2,18},{3,19},{4,20},{5,21},{6,22},{7,23},{8,24},{9,... | collective-permute-start | bytes 393224 | tf_op jit(solution)/shard_map/ppermute | solution.py:28
  106.8 5.3 %collective-permute-start.20 = (bf16[256,512]{1,0:T(8,128)(2,1)S(1)}, bf16[256,512]{1,0:T(8,128)(2,1)S(1)}, u32[]{:S(2)}, u32[]{:S(2)}) collective-permute-start(bf16[256,512]{1,0:T(8,128)(2,1)S(1)} %get-tuple-element.29), channel_id=1, source_target_pairs={{0,1},{1,0},{2,3},{3,2},{4,5},{5,4},{6,7},{7,6},{8,9},{9,8},{10,11... | collective-permute-start | bytes 786440 | tf_op jit(solution)/shard_map/ppermute | solution.py:28
  114.0 10.3 %all-to-all-start = ((bf16[32,8,512]{2,1,0:T(8,128)(2,1)}), bf16[32,8,512]{2,1,0:T(8,128)(2,1)S(1)}, u32[]{:S(2)}, u32[]{:S(2)}) async-start(bf16[32,8,512]{2,1,0:T(8,128)(2,1)} %weight_half.1), calls=%async_computation | async-start | bytes 524288 | tf_op jit(solution)/shard_map/all_to_all | solution.py:247
  124.3 2.7 %collective-permute-start.21 = (bf16[2,128,512]{2,1,0:T(8,128)(2,1)S(1)}, bf16[2,128,512]{2,1,0:T(8,128)(2,1)S(1)}, u32[]{:S(2)}, u32[]{:S(2)}) collective-permute-start(bf16[2,128,512]{2,1,0:T(8,128)(2,1)S(1)} %get-tuple-element.30), channel_id=1, source_target_pairs={{0,16},{1,17},{2,18},{3,19},{4,20},{5,21},{6,22},{7,23},{8,24},{9,... | collective-permute-start | bytes 786440 | tf_op jit(solution)/shard_map/ppermute | solution.py:28
  127.0 6.4 %collective-permute-done.21.came = bf16[2,128,512]{2,1,0:T(8,128)(2,1)S(1)} collective-permute-done((bf16[2,128,512]{2,1,0:T(8,128)(2,1)S(1)}, bf16[2,128,512]{2,1,0:T(8,128)(2,1)S(1)}, u32[]{:S(2)}, u32[]{:S(2)}) %collective-permute-start.21) | collective-permute-done | bytes 262176 | tf_op jit(solution)/shard_map/ppermute | solution.py:28
  133.4 2.5 %all-to-all-done.half = bf16[32,8,512]{2,1,0:T(8,128)(2,1)S(1)} async-done(((bf16[32,8,512]{2,1,0:T(8,128)(2,1)}), bf16[32,8,512]{2,1,0:T(8,128)(2,1)S(1)}, u32[]{:S(2)}, u32[]{:S(2)}) %all-to-all-start) | async-done | bytes 262176 | tf_op jit(solution)/shard_map/all_to_all | solution.py:247
  136.5 5.4 %collective-permute-start.22 = (bf16[128,512]{1,0:T(8,128)(2,1)S(1)}, bf16[128,512]{1,0:T(8,128)(2,1)S(1)}, u32[]{:S(2)}, u32[]{:S(2)}) collective-permute-start(bf16[128,512]{1,0:T(8,128)(2,1)S(1)} %get-tuple-element.33), channel_id=1, source_target_pairs={{0,32},{1,33},{2,34},{3,35},{4,36},{5,37},{6,38},{7,39},{8,40},{9,... | collective-permute-start | bytes 393224 | tf_op jit(solution)/shard_map/ppermute | solution.py:28
  141.9 9.0 %all_to_all.15.share = bf16[8,8,512]{2,1,0:T(8,128)(2,1)S(1)} all-to-all(bf16[8,8,512]{2,1,0:T(8,128)(2,1)S(1)} %get-tuple-element.31), channel_id=1, replica_groups=mesh['z'=8,'y'=4,'x'=4,'h'=2,'k'=2] {'y','h'}, dimensions={0} | all-to-all | bytes 131072 | tf_op jit(solution)/shard_map/all_to_all | solution.py:259
  151.9 16.7 %all_to_all.16.own = bf16[32,8,512]{2,1,0:T(8,128)(2,1)S(1)} all-to-all(bf16[32,8,512]{2,1,0:T(8,128)(2,1)S(1)} %get-tuple-element.35), channel_id=1, replica_groups=mesh['z'=8,'y'=4,'x'=4,'h'=2,'k'=2] {'z','x'}, dimensions={0} | all-to-all | bytes 524288 | tf_op jit(solution)/shard_map/all_to_all | solution.py:266
  168.6 6.4 %collective-permute-start.23 = (bf16[32,8,512]{2,1,0:T(8,128)(2,1)S(1)}, bf16[32,8,512]{2,1,0:T(8,128)(2,1)S(1)}, u32[]{:S(2)}, u32[]{:S(2)}) collective-permute-start(bf16[32,8,512]{2,1,0:T(8,128)(2,1)S(1)} %all_to_all.16.own), channel_id=1, source_target_pairs={{0,1},{1,0},{2,3},{3,2},{4,5},{5,4},{6,7},{7,6},{8,9},{9,8},{10,11... | collective-permute-start | bytes 786440 | tf_op jit(solution)/shard_map/ppermute | solution.py:28
  (45 shorter events, 14.8 us)
Async XLA Ops:
  1.7 19.5 %collective-permute-start.6 = (bf16[128,512]{1,0:T(8,128)(2,1)S(1)}, bf16[128,512]{1,0:T(8,128)(2,1)S(1)}, u32[]{:S(2)}, u32[]{:S(2)}) collective-permute-start(bf16[128,512]{1,0:T(8,128)(2,1)S(1)} %multiply_convert_fusion), channel_id=1, source_target_pairs={{0,2},{1,3},{2,0},{3,1},{4,6},{5,7},{6,4},{7,5},{8,10},{9,11},{10,... | collective-permute-start | bytes 393224 | tf_op jit(solution)/shard_map/ppermute | solution.py:28
  9.9 15.9 %collective-permute-start.4 = (bf16[128,512]{1,0:T(8,128)(2,1)S(1)}, bf16[128,512]{1,0:T(8,128)(2,1)S(1)}, u32[]{:S(2)}, u32[]{:S(2)}) collective-permute-start(bf16[128,512]{1,0:T(8,128)(2,1)S(1)} %multiply_convert_fusion), channel_id=1, source_target_pairs={{0,8},{1,9},{2,10},{3,11},{4,12},{5,13},{6,14},{7,15},{8,0},{9,1},... | collective-permute-start | bytes 393224 | tf_op jit(solution)/shard_map/ppermute | solution.py:28
  14.6 13.8 %collective-permute-start.5 = (bf16[128,512]{1,0:T(8,128)(2,1)S(1)}, bf16[128,512]{1,0:T(8,128)(2,1)S(1)}, u32[]{:S(2)}, u32[]{:S(2)}) collective-permute-start(bf16[128,512]{1,0:T(8,128)(2,1)S(1)} %multiply_convert_fusion), channel_id=1, source_target_pairs={{0,4},{1,5},{2,6},{3,7},{4,8},{5,9},{6,10},{7,11},{8,12},{9,13},{1... | collective-permute-start | bytes 393224 | tf_op jit(solution)/shard_map/ppermute | solution.py:28
  16.8 11.5 %collective-permute-start.3 = (bf16[128,512]{1,0:T(8,128)(2,1)S(1)}, bf16[128,512]{1,0:T(8,128)(2,1)S(1)}, u32[]{:S(2)}, u32[]{:S(2)}) collective-permute-start(bf16[128,512]{1,0:T(8,128)(2,1)S(1)} %multiply_convert_fusion), channel_id=1, source_target_pairs={{0,12},{1,13},{2,14},{3,15},{4,0},{5,1},{6,2},{7,3},{8,4},{9,5},{1... | collective-permute-start | bytes 393224 | tf_op jit(solution)/shard_map/ppermute | solution.py:28
  21.1 11.6 %collective-permute-start.7 = (bf16[128,512]{1,0:T(8,128)(2,1)S(1)}, bf16[128,512]{1,0:T(8,128)(2,1)S(1)}, u32[]{:S(2)}, u32[]{:S(2)}) collective-permute-start(bf16[128,512]{1,0:T(8,128)(2,1)S(1)} %collective-permute-done.6), channel_id=1, source_target_pairs={{0,12},{1,13},{2,14},{3,15},{4,0},{5,1},{6,2},{7,3},{8,4},{9,5},{1... | collective-permute-start | bytes 393224 | tf_op jit(solution)/shard_map/ppermute | solution.py:28
  23.0 9.7 %collective-permute-start.8 = (bf16[128,512]{1,0:T(8,128)(2,1)S(1)}, bf16[128,512]{1,0:T(8,128)(2,1)S(1)}, u32[]{:S(2)}, u32[]{:S(2)}) collective-permute-start(bf16[128,512]{1,0:T(8,128)(2,1)S(1)} %collective-permute-done.6), channel_id=1, source_target_pairs={{0,8},{1,9},{2,10},{3,11},{4,12},{5,13},{6,14},{7,15},{8,0},{9,1},... | collective-permute-start | bytes 393224 | tf_op jit(solution)/shard_map/ppermute | solution.py:28
  25.9 8.1 %collective-permute-start.9 = (bf16[128,512]{1,0:T(8,128)(2,1)S(1)}, bf16[128,512]{1,0:T(8,128)(2,1)S(1)}, u32[]{:S(2)}, u32[]{:S(2)}) collective-permute-start(bf16[128,512]{1,0:T(8,128)(2,1)S(1)} %collective-permute-done.6), channel_id=1, source_target_pairs={{0,4},{1,5},{2,6},{3,7},{4,8},{5,9},{6,10},{7,11},{8,12},{9,13},{1... | collective-permute-start | bytes 393224 | tf_op jit(solution)/shard_map/ppermute | solution.py:28
  28.5 11.3 %collective-permute-start.10 = (bf16[4,128,512]{2,1,0:T(8,128)(2,1)S(1)}, bf16[4,128,512]{2,1,0:T(8,128)(2,1)S(1)}, u32[]{:S(2)}, u32[]{:S(2)}) collective-permute-start(bf16[4,128,512]{2,1,0:T(8,128)(2,1)S(1)} %pad_maximum_fusion.own), channel_id=1, source_target_pairs={{0,1},{1,0},{2,3},{3,2},{4,5},{5,4},{6,7},{7,6},{8,9},{9,8},{10,11... | collective-permute-start | bytes 1572872 | tf_op jit(solution)/shard_map/ppermute | solution.py:28
  34.0 5.8 %collective-permute-start.11 = (bf16[4,128,512]{2,1,0:T(8,128)(2,1)S(1)}, bf16[4,128,512]{2,1,0:T(8,128)(2,1)S(1)}, u32[]{:S(2)}, u32[]{:S(2)}) collective-permute-start(bf16[4,128,512]{2,1,0:T(8,128)(2,1)S(1)} %pad_maximum_fusion.1.own_h), channel_id=1, source_target_pairs={{0,1},{1,0},{2,3},{3,2},{4,5},{5,4},{6,7},{7,6},{8,9},{9,8},{10,11... | collective-permute-start | bytes 1572872 | tf_op jit(solution)/shard_map/ppermute | solution.py:28
  39.8 0.8 copy-start.2
  40.6 26.6 %copy-start.1 = (bf16[128,512]{1,0:T(8,128)(2,1)S(1)}, bf16[128,512]{1,0:T(8,128)(2,1)}, u32[]{:S(2)}) copy-start(bf16[128,512]{1,0:T(8,128)(2,1)} %features.1) | copy-start | bytes 393220
  44.6 15.9 %collective-permute-start.12 = (bf16[4,64,512]{2,1,0:T(8,128)(2,1)S(1)}, bf16[4,64,512]{2,1,0:T(8,128)(2,1)S(1)}, u32[]{:S(2)}, u32[]{:S(2)}) collective-permute-start(bf16[4,64,512]{2,1,0:T(8,128)(2,1)S(1)} %get-tuple-element.23), channel_id=1, source_target_pairs={{0,64},{1,65},{2,66},{3,67},{4,68},{5,69},{6,70},{7,71},{8,72},{9,... | collective-permute-start | bytes 786440 | tf_op jit(solution)/shard_map/ppermute | solution.py:28
  48.6 13.9 %collective-permute-start.16 = (bf16[4,64,512]{2,1,0:T(8,128)(2,1)S(1)}, bf16[4,64,512]{2,1,0:T(8,128)(2,1)S(1)}, u32[]{:S(2)}, u32[]{:S(2)}) collective-permute-start(bf16[4,64,512]{2,1,0:T(8,128)(2,1)S(1)} %get-tuple-element.27), channel_id=1, source_target_pairs={{0,448},{1,449},{2,450},{3,451},{4,452},{5,453},{6,454},{7,455},{8... | collective-permute-start | bytes 786440 | tf_op jit(solution)/shard_map/ppermute | solution.py:28
  60.6 14.5 %collective-permute-start.13 = (bf16[4,128,512]{2,1,0:T(8,128)(2,1)S(1)}, bf16[4,128,512]{2,1,0:T(8,128)(2,1)S(1)}, u32[]{:S(2)}, u32[]{:S(2)}) collective-permute-start(bf16[4,128,512]{2,1,0:T(8,128)(2,1)S(1)} %ring_add.6), channel_id=1, source_target_pairs={{0,64},{1,65},{2,66},{3,67},{4,68},{5,69},{6,70},{7,71},{8,72},{9,... | collective-permute-start | bytes 1572872 | tf_op jit(solution)/shard_map/ppermute | solution.py:28
  62.6 14.6 %collective-permute-start.17 = (bf16[4,128,512]{2,1,0:T(8,128)(2,1)S(1)}, bf16[4,128,512]{2,1,0:T(8,128)(2,1)S(1)}, u32[]{:S(2)}, u32[]{:S(2)}) collective-permute-start(bf16[4,128,512]{2,1,0:T(8,128)(2,1)S(1)} %ring_add.9), channel_id=1, source_target_pairs={{0,448},{1,449},{2,450},{3,451},{4,452},{5,453},{6,454},{7,455},{8... | collective-permute-start | bytes 1572872 | tf_op jit(solution)/shard_map/ppermute | solution.py:28
  67.2 10.0 %collective-permute-start = (bf16[128,512]{1,0:T(8,128)(2,1)S(1)}, bf16[128,512]{1,0:T(8,128)(2,1)S(1)}, u32[]{:S(2)}, u32[]{:S(2)}) collective-permute-start(bf16[128,512]{1,0:T(8,128)(2,1)S(1)} %copy-done.1), channel_id=1, source_target_pairs={{0,48},{1,49},{2,50},{3,51},{4,52},{5,53},{6,54},{7,55},{8,56},{9,... | collective-permute-start | bytes 393224 | tf_op jit(solution)/shard_map/ppermute | solution.py:28
  75.2 13.6 %collective-permute-start.14 = (bf16[4,128,512]{2,1,0:T(8,128)(2,1)S(1)}, bf16[4,128,512]{2,1,0:T(8,128)(2,1)S(1)}, u32[]{:S(2)}, u32[]{:S(2)}) collective-permute-start(bf16[4,128,512]{2,1,0:T(8,128)(2,1)S(1)} %ring_add.7), channel_id=1, source_target_pairs={{0,64},{1,65},{2,66},{3,67},{4,68},{5,69},{6,70},{7,71},{8,72},{9,... | collective-permute-start | bytes 1572872 | tf_op jit(solution)/shard_map/ppermute | solution.py:28
  77.3 13.6 %collective-permute-start.18 = (bf16[4,128,512]{2,1,0:T(8,128)(2,1)S(1)}, bf16[4,128,512]{2,1,0:T(8,128)(2,1)S(1)}, u32[]{:S(2)}, u32[]{:S(2)}) collective-permute-start(bf16[4,128,512]{2,1,0:T(8,128)(2,1)S(1)} %ring_add.10), channel_id=1, source_target_pairs={{0,448},{1,449},{2,450},{3,451},{4,452},{5,453},{6,454},{7,455},{8... | collective-permute-start | bytes 1572872 | tf_op jit(solution)/shard_map/ppermute | solution.py:28
  81.9 9.0 %collective-permute-start.1 = (bf16[128,512]{1,0:T(8,128)(2,1)S(1)}, bf16[128,512]{1,0:T(8,128)(2,1)S(1)}, u32[]{:S(2)}, u32[]{:S(2)}) collective-permute-start(bf16[128,512]{1,0:T(8,128)(2,1)S(1)} %copy-done.1), channel_id=1, source_target_pairs={{0,32},{1,33},{2,34},{3,35},{4,36},{5,37},{6,38},{7,39},{8,40},{9,... | collective-permute-start | bytes 393224 | tf_op jit(solution)/shard_map/ppermute | solution.py:28
  89.0 14.6 %collective-permute-start.15 = (bf16[4,128,512]{2,1,0:T(8,128)(2,1)S(1)}, bf16[4,128,512]{2,1,0:T(8,128)(2,1)S(1)}, u32[]{:S(2)}, u32[]{:S(2)}) collective-permute-start(bf16[4,128,512]{2,1,0:T(8,128)(2,1)S(1)} %ring_add.8), channel_id=1, source_target_pairs={{0,64},{1,65},{2,66},{3,67},{4,68},{5,69},{6,70},{7,71},{8,72},{9,... | collective-permute-start | bytes 1572872 | tf_op jit(solution)/shard_map/ppermute | solution.py:28
  91.1 59.8 %copy-start = (bf16[512,512]{1,0:T(8,128)(2,1)S(1)}, bf16[512,512]{1,0:T(8,128)(2,1)}, u32[]{:S(2)}) copy-start(bf16[512,512]{1,0:T(8,128)(2,1)} %weight.1) | copy-start | bytes 1572868
  91.1 12.5 %collective-permute-start.19 = (bf16[4,128,512]{2,1,0:T(8,128)(2,1)S(1)}, bf16[4,128,512]{2,1,0:T(8,128)(2,1)S(1)}, u32[]{:S(2)}, u32[]{:S(2)}) collective-permute-start(bf16[4,128,512]{2,1,0:T(8,128)(2,1)S(1)} %ring_add.11), channel_id=1, source_target_pairs={{0,448},{1,449},{2,450},{3,451},{4,452},{5,453},{6,454},{7,455},{8... | collective-permute-start | bytes 1572872 | tf_op jit(solution)/shard_map/ppermute | solution.py:28
  95.8 9.7 %collective-permute-start.2 = (bf16[128,512]{1,0:T(8,128)(2,1)S(1)}, bf16[128,512]{1,0:T(8,128)(2,1)S(1)}, u32[]{:S(2)}, u32[]{:S(2)}) collective-permute-start(bf16[128,512]{1,0:T(8,128)(2,1)S(1)} %copy-done.1), channel_id=1, source_target_pairs={{0,16},{1,17},{2,18},{3,19},{4,20},{5,21},{6,22},{7,23},{8,24},{9,... | collective-permute-start | bytes 393224 | tf_op jit(solution)/shard_map/ppermute | solution.py:28
  106.8 6.4 %collective-permute-start.20 = (bf16[256,512]{1,0:T(8,128)(2,1)S(1)}, bf16[256,512]{1,0:T(8,128)(2,1)S(1)}, u32[]{:S(2)}, u32[]{:S(2)}) collective-permute-start(bf16[256,512]{1,0:T(8,128)(2,1)S(1)} %get-tuple-element.29), channel_id=1, source_target_pairs={{0,1},{1,0},{2,3},{3,2},{4,5},{5,4},{6,7},{7,6},{8,9},{9,8},{10,11... | collective-permute-start | bytes 786440 | tf_op jit(solution)/shard_map/ppermute | solution.py:28
  114.0 21.9 %all-to-all-start = ((bf16[32,8,512]{2,1,0:T(8,128)(2,1)}), bf16[32,8,512]{2,1,0:T(8,128)(2,1)S(1)}, u32[]{:S(2)}, u32[]{:S(2)}) async-start(bf16[32,8,512]{2,1,0:T(8,128)(2,1)} %weight_half.1), calls=%async_computation | async-start | bytes 524288 | tf_op jit(solution)/shard_map/all_to_all | solution.py:247
  124.3 9.1 %collective-permute-start.21 = (bf16[2,128,512]{2,1,0:T(8,128)(2,1)S(1)}, bf16[2,128,512]{2,1,0:T(8,128)(2,1)S(1)}, u32[]{:S(2)}, u32[]{:S(2)}) collective-permute-start(bf16[2,128,512]{2,1,0:T(8,128)(2,1)S(1)} %get-tuple-element.30), channel_id=1, source_target_pairs={{0,16},{1,17},{2,18},{3,19},{4,20},{5,21},{6,22},{7,23},{8,24},{9,... | collective-permute-start | bytes 786440 | tf_op jit(solution)/shard_map/ppermute | solution.py:28
  136.5 14.4 %collective-permute-start.22 = (bf16[128,512]{1,0:T(8,128)(2,1)S(1)}, bf16[128,512]{1,0:T(8,128)(2,1)S(1)}, u32[]{:S(2)}, u32[]{:S(2)}) collective-permute-start(bf16[128,512]{1,0:T(8,128)(2,1)S(1)} %get-tuple-element.33), channel_id=1, source_target_pairs={{0,32},{1,33},{2,34},{3,35},{4,36},{5,37},{6,38},{7,39},{8,40},{9,... | collective-permute-start | bytes 393224 | tf_op jit(solution)/shard_map/ppermute | solution.py:28
  168.6 7.6 %collective-permute-start.23 = (bf16[32,8,512]{2,1,0:T(8,128)(2,1)S(1)}, bf16[32,8,512]{2,1,0:T(8,128)(2,1)S(1)}, u32[]{:S(2)}, u32[]{:S(2)}) collective-permute-start(bf16[32,8,512]{2,1,0:T(8,128)(2,1)S(1)} %all_to_all.16.own), channel_id=1, source_target_pairs={{0,1},{1,0},{2,3},{3,2},{4,5},{5,4},{6,7},{7,6},{8,9},{9,8},{10,11... | collective-permute-start | bytes 786440 | tf_op jit(solution)/shard_map/ppermute | solution.py:28

commit v4 on v3

--- a/solution.py
+++ b/solution.py
@@ -104,7 +104,7 @@
             acc[row] += term
         return carry
 
-    lax.fori_loop(0, pl.cdiv(codes[SLOTS], UNROLL), group, 0)
+    lax.fori_loop(0, pl.cdiv(at[3], UNROLL), group, 0)
 
     def chunk(step, rows=slice(None)):
         return acc[pl.ds(4 * lax.rem(at[0] + step, 8), 4), rows].astype(jnp.bfloat16)
@@ -196,8 +196,8 @@
     places = (cols // 4 - x) % 4 + 4 * ((cols // 2 % 2) ^ h) + 8 * ((cols % 2) ^ k)
 
     live = jnp.arange(SLOTS, dtype=jnp.int32) < tile_count[0, 0]
-    codes = jnp.concatenate([jnp.where(live, tile_rows[0, 0] * 16 + places, 32 * 16), tile_count[0]])
-    at = jnp.stack([lax.axis_index("z"), lax.axis_index("y"), k])
+    codes = jnp.where(live, tile_rows[0, 0] * 16 + places, 32 * 16)
+    at = jnp.stack([lax.axis_index("z"), lax.axis_index("y"), k, tile_count[0, 0]])
     piece = jax.ShapeDtypeStruct((4, 128, WIDTH), jnp.bfloat16)
     first = [
         jax.ShapeDtypeStruct((4, HALF, WIDTH), jnp.bfloat16),

time: 179 us -> 180 us (level)
  blocking collectives: 25.7 us -> 29 us
  starting transfers between devices: 115 us -> 112 us
    ppermute x24, starting transfers between devices: 105 us -> 101 us  [permute(): return lax.ppermute(value, AXES, pairs)]
    all_to_all x1, blocking collectives: 9.02 us -> 12.3 us  [body(): share = lax.all_to_all(share, ('y', 'h'), 0, 0, tiled=True)]
    ppermute x24, waiting for transfers between devices: 19.9 us -> 21.9 us  [permute(): return lax.ppermute(value, AXES, pairs)]
  transfers between devices with their start and end apart: 25 -> 25, of which waited for: 9 -> 11; matrix products, arithmetic and copies ran while one was open for 1% -> 1% of each run, Pallas kernels for 0% -> 0%
where the time goes in v4:
time: 180 us; the launch traced here: 179 us
  starting transfers between devices  112 us (62%)
  blocking collectives  29 us (16%)
  waiting for transfers between devices  23 us (13%)
  Pallas kernels  10.8 us (6%)
  other arithmetic  2.14 us (1%)
    ppermute x24, starting transfers between devices, permute(): return lax.ppermute(value, AXES, pairs)  101 us
    ppermute x24, waiting for transfers between devices, permute(): return lax.ppermute(value, AXES, pairs)  21.9 us
    all_to_all x1, blocking collectives, body(): half = lax.all_to_all(half, ('z', 'x'), 0, 0, tiled=True)  16.7 us
    all_to_all x1, blocking collectives, body(): share = lax.all_to_all(share, ('y', 'h'), 0, 0, tiled=True)  12.3 us
    all_to_all x1, starting transfers between devices, body(): half = lax.all_to_all(half, ('z', 'x'), 0, 0, tiled=True)  11.1 us
    pallas_call x1, Pallas kernels, body(): kernel_call(block_kernel, first + [piece] * 7, [SMEM_SPEC] * 2 + [pl.Bloc...  4.93 us
  transfers between devices with their start and end apart: 25, of which 11 were waited for; matrix products, arithmetic and copies ran while one was open for 1% of the time, Pallas kernels for 0%

profile of v4, /device:TPU:1, one launch (start us, length us, event | category | flops | bytes accessed | tf_op | source)
XLA Modules:
  0.0 179.2 jit_solution(2713535246522682845)
XLA Ops:
  1.7 8.3 %collective-permute-start.6 = (bf16[128,512]{1,0:T(8,128)(2,1)S(1)}, bf16[128,512]{1,0:T(8,128)(2,1)S(1)}, u32[]{:S(2)}, u32[]{:S(2)}) collective-permute-start(bf16[128,512]{1,0:T(8,128)(2,1)S(1)} %multiply_convert_fusion), channel_id=1, source_target_pairs={{0,2},{1,3},{2,0},{3,1},{4,6},{5,7},{6,4},{7,5},{8,10},{9,11},{10,... | collective-permute-start | bytes 393224 | tf_op jit(solution)/shard_map/ppermute | solution.py:28
  9.9 4.7 %collective-permute-start.4 = (bf16[128,512]{1,0:T(8,128)(2,1)S(1)}, bf16[128,512]{1,0:T(8,128)(2,1)S(1)}, u32[]{:S(2)}, u32[]{:S(2)}) collective-permute-start(bf16[128,512]{1,0:T(8,128)(2,1)S(1)} %multiply_convert_fusion), channel_id=1, source_target_pairs={{0,8},{1,9},{2,10},{3,11},{4,12},{5,13},{6,14},{7,15},{8,0},{9,1},... | collective-permute-start | bytes 393224 | tf_op jit(solution)/shard_map/ppermute | solution.py:28
  14.6 2.2 %collective-permute-start.5 = (bf16[128,512]{1,0:T(8,128)(2,1)S(1)}, bf16[128,512]{1,0:T(8,128)(2,1)S(1)}, u32[]{:S(2)}, u32[]{:S(2)}) collective-permute-start(bf16[128,512]{1,0:T(8,128)(2,1)S(1)} %multiply_convert_fusion), channel_id=1, source_target_pairs={{0,4},{1,5},{2,6},{3,7},{4,8},{5,9},{6,10},{7,11},{8,12},{9,13},{1... | collective-permute-start | bytes 393224 | tf_op jit(solution)/shard_map/ppermute | solution.py:28
  16.8 4.3 %collective-permute-start.3 = (bf16[128,512]{1,0:T(8,128)(2,1)S(1)}, bf16[128,512]{1,0:T(8,128)(2,1)S(1)}, u32[]{:S(2)}, u32[]{:S(2)}) collective-permute-start(bf16[128,512]{1,0:T(8,128)(2,1)S(1)} %multiply_convert_fusion), channel_id=1, source_target_pairs={{0,12},{1,13},{2,14},{3,15},{4,0},{5,1},{6,2},{7,3},{8,4},{9,5},{1... | collective-permute-start | bytes 393224 | tf_op jit(solution)/shard_map/ppermute | solution.py:28
  21.1 1.9 %collective-permute-start.7 = (bf16[128,512]{1,0:T(8,128)(2,1)S(1)}, bf16[128,512]{1,0:T(8,128)(2,1)S(1)}, u32[]{:S(2)}, u32[]{:S(2)}) collective-permute-start(bf16[128,512]{1,0:T(8,128)(2,1)S(1)} %collective-permute-done.6), channel_id=1, source_target_pairs={{0,12},{1,13},{2,14},{3,15},{4,0},{5,1},{6,2},{7,3},{8,4},{9,5},{1... | collective-permute-start | bytes 393224 | tf_op jit(solution)/shard_map/ppermute | solution.py:28
  23.0 2.8 %collective-permute-start.8 = (bf16[128,512]{1,0:T(8,128)(2,1)S(1)}, bf16[128,512]{1,0:T(8,128)(2,1)S(1)}, u32[]{:S(2)}, u32[]{:S(2)}) collective-permute-start(bf16[128,512]{1,0:T(8,128)(2,1)S(1)} %collective-permute-done.6), channel_id=1, source_target_pairs={{0,8},{1,9},{2,10},{3,11},{4,12},{5,13},{6,14},{7,15},{8,0},{9,1},... | collective-permute-start | bytes 393224 | tf_op jit(solution)/shard_map/ppermute | solution.py:28
  25.9 2.5 %collective-permute-start.9 = (bf16[128,512]{1,0:T(8,128)(2,1)S(1)}, bf16[128,512]{1,0:T(8,128)(2,1)S(1)}, u32[]{:S(2)}, u32[]{:S(2)}) collective-permute-start(bf16[128,512]{1,0:T(8,128)(2,1)S(1)} %collective-permute-done.6), channel_id=1, source_target_pairs={{0,4},{1,5},{2,6},{3,7},{4,8},{5,9},{6,10},{7,11},{8,12},{9,13},{1... | collective-permute-start | bytes 393224 | tf_op jit(solution)/shard_map/ppermute | solution.py:28
  28.5 4.3 %collective-permute-start.10 = (bf16[4,128,512]{2,1,0:T(8,128)(2,1)S(1)}, bf16[4,128,512]{2,1,0:T(8,128)(2,1)S(1)}, u32[]{:S(2)}, u32[]{:S(2)}) collective-permute-start(bf16[4,128,512]{2,1,0:T(8,128)(2,1)S(1)} %pad_maximum_fusion.own), channel_id=1, source_target_pairs={{0,1},{1,0},{2,3},{3,2},{4,5},{5,4},{6,7},{7,6},{8,9},{9,8},{10,11... | collective-permute-start | bytes 1572872 | tf_op jit(solution)/shard_map/ppermute | solution.py:28
  34.0 4.3 %collective-permute-start.11 = (bf16[4,128,512]{2,1,0:T(8,128)(2,1)S(1)}, bf16[4,128,512]{2,1,0:T(8,128)(2,1)S(1)}, u32[]{:S(2)}, u32[]{:S(2)}) collective-permute-start(bf16[4,128,512]{2,1,0:T(8,128)(2,1)S(1)} %pad_maximum_fusion.1.own_h), channel_id=1, source_target_pairs={{0,1},{1,0},{2,3},{3,2},{4,5},{5,4},{6,7},{7,6},{8,9},{9,8},{10,11... | collective-permute-start | bytes 1572872 | tf_op jit(solution)/shard_map/ppermute | solution.py:28
  40.6 4.9 %block_terms.1 = (bf16[4,64,512]{2,1,0:T(8,128)(2,1)S(1)}, bf16[4,64,512]{2,1,0:T(8,128)(2,1)S(1)}, bf16[4,128,512]{2,1,0:T(8,128)(2,1)S(1)}, bf16[4,128,512]{2,...) custom-call(s32[4]{0:T(128)S(1)} %pad_add_fusion.at, ...), custom_call_target="tpu_custom_call" | custom-call | tf_op jit(solution)/shard_map/block_terms/pallas_call | solution.py:206
  45.5 3.0 %collective-permute-start.12 = (bf16[4,64,512]{2,1,0:T(8,128)(2,1)S(1)}, bf16[4,64,512]{2,1,0:T(8,128)(2,1)S(1)}, u32[]{:S(2)}, u32[]{:S(2)}) collective-permute-start(bf16[4,64,512]{2,1,0:T(8,128)(2,1)S(1)} %get-tuple-element.23), channel_id=1, source_target_pairs={{0,64},{1,65},{2,66},{3,67},{4,68},{5,69},{6,70},{7,71},{8,72},{9,... | collective-permute-start | bytes 786440 | tf_op jit(solution)/shard_map/ppermute | solution.py:28
  48.6 8.6 %collective-permute-start.16 = (bf16[4,64,512]{2,1,0:T(8,128)(2,1)S(1)}, bf16[4,64,512]{2,1,0:T(8,128)(2,1)S(1)}, u32[]{:S(2)}, u32[]{:S(2)}) collective-permute-start(bf16[4,64,512]{2,1,0:T(8,128)(2,1)S(1)} %get-tuple-element.27), channel_id=1, source_target_pairs={{0,448},{1,449},{2,450},{3,451},{4,452},{5,453},{6,454},{7,455},{8... | collective-permute-start | bytes 786440 | tf_op jit(solution)/shard_map/ppermute | solution.py:28
  57.2 3.3 %collective-permute-done.12.came = bf16[4,64,512]{2,1,0:T(8,128)(2,1)S(1)} collective-permute-done((bf16[4,64,512]{2,1,0:T(8,128)(2,1)S(1)}, bf16[4,64,512]{2,1,0:T(8,128)(2,1)S(1)}, u32[]{:S(2)}, u32[]{:S(2)}) %collective-permute-start.12) | collective-permute-done | bytes 262176 | tf_op jit(solution)/shard_map/ppermute | solution.py:28
  60.6 1.9 %collective-permute-start.13 = (bf16[4,128,512]{2,1,0:T(8,128)(2,1)S(1)}, bf16[4,128,512]{2,1,0:T(8,128)(2,1)S(1)}, u32[]{:S(2)}, u32[]{:S(2)}) collective-permute-start(bf16[4,128,512]{2,1,0:T(8,128)(2,1)S(1)} %ring_add.6), channel_id=1, source_target_pairs={{0,64},{1,65},{2,66},{3,67},{4,68},{5,69},{6,70},{7,71},{8,72},{9,... | collective-permute-start | bytes 1572872 | tf_op jit(solution)/shard_map/ppermute | solution.py:28
  62.6 4.6 %collective-permute-start.17 = (bf16[4,128,512]{2,1,0:T(8,128)(2,1)S(1)}, bf16[4,128,512]{2,1,0:T(8,128)(2,1)S(1)}, u32[]{:S(2)}, u32[]{:S(2)}) collective-permute-start(bf16[4,128,512]{2,1,0:T(8,128)(2,1)S(1)} %ring_add.9), channel_id=1, source_target_pairs={{0,448},{1,449},{2,450},{3,451},{4,452},{5,453},{6,454},{7,455},{8... | collective-permute-start | bytes 1572872 | tf_op jit(solution)/shard_map/ppermute | solution.py:28
  67.2 3.7 %collective-permute-start = (bf16[128,512]{1,0:T(8,128)(2,1)S(1)}, bf16[128,512]{1,0:T(8,128)(2,1)S(1)}, u32[]{:S(2)}, u32[]{:S(2)}) collective-permute-start(bf16[128,512]{1,0:T(8,128)(2,1)S(1)} %copy-done.1), channel_id=1, source_target_pairs={{0,48},{1,49},{2,50},{3,51},{4,52},{5,53},{6,54},{7,55},{8,56},{9,... | collective-permute-start | bytes 393224 | tf_op jit(solution)/shard_map/ppermute | solution.py:28
  70.9 4.2 %collective-permute-done.13.came = bf16[4,128,512]{2,1,0:T(8,128)(2,1)S(1)} collective-permute-done((bf16[4,128,512]{2,1,0:T(8,128)(2,1)S(1)}, bf16[4,128,512]{2,1,0:T(8,128)(2,1)S(1)}, u32[]{:S(2)}, u32[]{:S(2)}) %collective-permute-start.13) | collective-permute-done | bytes 524320 | tf_op jit(solution)/shard_map/ppermute | solution.py:28
  75.2 1.9 %collective-permute-start.14 = (bf16[4,128,512]{2,1,0:T(8,128)(2,1)S(1)}, bf16[4,128,512]{2,1,0:T(8,128)(2,1)S(1)}, u32[]{:S(2)}, u32[]{:S(2)}) collective-permute-start(bf16[4,128,512]{2,1,0:T(8,128)(2,1)S(1)} %ring_add.7), channel_id=1, source_target_pairs={{0,64},{1,65},{2,66},{3,67},{4,68},{5,69},{6,70},{7,71},{8,72},{9,... | collective-permute-start | bytes 1572872 | tf_op jit(solution)/shard_map/ppermute | solution.py:28
  77.3 4.7 %collective-permute-start.18 = (bf16[4,128,512]{2,1,0:T(8,128)(2,1)S(1)}, bf16[4,128,512]{2,1,0:T(8,128)(2,1)S(1)}, u32[]{:S(2)}, u32[]{:S(2)}) collective-permute-start(bf16[4,128,512]{2,1,0:T(8,128)(2,1)S(1)} %ring_add.10), channel_id=1, source_target_pairs={{0,448},{1,449},{2,450},{3,451},{4,452},{5,453},{6,454},{7,455},{8... | collective-permute-start | bytes 1572872 | tf_op jit(solution)/shard_map/ppermute | solution.py:28
  82.0 7.5 %collective-permute-start.1 = (bf16[128,512]{1,0:T(8,128)(2,1)S(1)}, bf16[128,512]{1,0:T(8,128)(2,1)S(1)}, u32[]{:S(2)}, u32[]{:S(2)}) collective-permute-start(bf16[128,512]{1,0:T(8,128)(2,1)S(1)} %copy-done.1), channel_id=1, source_target_pairs={{0,32},{1,33},{2,34},{3,35},{4,36},{5,37},{6,38},{7,39},{8,40},{9,... | collective-permute-start | bytes 393224 | tf_op jit(solution)/shard_map/ppermute | solution.py:28
  89.6 1.9 %collective-permute-start.15 = (bf16[4,128,512]{2,1,0:T(8,128)(2,1)S(1)}, bf16[4,128,512]{2,1,0:T(8,128)(2,1)S(1)}, u32[]{:S(2)}, u32[]{:S(2)}) collective-permute-start(bf16[4,128,512]{2,1,0:T(8,128)(2,1)S(1)} %ring_add.8), channel_id=1, source_target_pairs={{0,64},{1,65},{2,66},{3,67},{4,68},{5,69},{6,70},{7,71},{8,72},{9,... | collective-permute-start | bytes 1572872 | tf_op jit(solution)/shard_map/ppermute | solution.py:28
  92.5 4.6 %collective-permute-start.19 = (bf16[4,128,512]{2,1,0:T(8,128)(2,1)S(1)}, bf16[4,128,512]{2,1,0:T(8,128)(2,1)S(1)}, u32[]{:S(2)}, u32[]{:S(2)}) collective-permute-start(bf16[4,128,512]{2,1,0:T(8,128)(2,1)S(1)} %ring_add.11), channel_id=1, source_target_pairs={{0,448},{1,449},{2,450},{3,451},{4,452},{5,453},{6,454},{7,455},{8... | collective-permute-start | bytes 1572872 | tf_op jit(solution)/shard_map/ppermute | solution.py:28
  97.1 4.4 %collective-permute-start.2 = (bf16[128,512]{1,0:T(8,128)(2,1)S(1)}, bf16[128,512]{1,0:T(8,128)(2,1)S(1)}, u32[]{:S(2)}, u32[]{:S(2)}) collective-permute-start(bf16[128,512]{1,0:T(8,128)(2,1)S(1)} %copy-done.1), channel_id=1, source_target_pairs={{0,16},{1,17},{2,18},{3,19},{4,20},{5,21},{6,22},{7,23},{8,24},{9,... | collective-permute-start | bytes 393224 | tf_op jit(solution)/shard_map/ppermute | solution.py:28
  101.5 2.7 %collective-permute-done.15 = bf16[4,128,512]{2,1,0:T(8,128)(2,1)S(1)} collective-permute-done((bf16[4,128,512]{2,1,0:T(8,128)(2,1)S(1)}, bf16[4,128,512]{2,1,0:T(8,128)(2,1)S(1)}, u32[]{:S(2)}, u32[]{:S(2)}) %collective-permute-start.15) | collective-permute-done | bytes 524320 | tf_op jit(solution)/shard_map/ppermute | solution.py:28
  107.0 5.7 %collective-permute-start.20 = (bf16[256,512]{1,0:T(8,128)(2,1)S(1)}, bf16[256,512]{1,0:T(8,128)(2,1)S(1)}, u32[]{:S(2)}, u32[]{:S(2)}) collective-permute-start(bf16[256,512]{1,0:T(8,128)(2,1)S(1)} %get-tuple-element.29), channel_id=1, source_target_pairs={{0,1},{1,0},{2,3},{3,2},{4,5},{5,4},{6,7},{7,6},{8,9},{9,8},{10,11... | collective-permute-start | bytes 786440 | tf_op jit(solution)/shard_map/ppermute | solution.py:28
  114.6 11.1 %all-to-all-start = ((bf16[32,8,512]{2,1,0:T(8,128)(2,1)}), bf16[32,8,512]{2,1,0:T(8,128)(2,1)S(1)}, u32[]{:S(2)}, u32[]{:S(2)}) async-start(bf16[32,8,512]{2,1,0:T(8,128)(2,1)} %weight_half.1), calls=%async_computation | async-start | bytes 524288 | tf_op jit(solution)/shard_map/all_to_all | solution.py:247
  125.7 4.4 %collective-permute-start.21 = (bf16[2,128,512]{2,1,0:T(8,128)(2,1)S(1)}, bf16[2,128,512]{2,1,0:T(8,128)(2,1)S(1)}, u32[]{:S(2)}, u32[]{:S(2)}) collective-permute-start(bf16[2,128,512]{2,1,0:T(8,128)(2,1)S(1)} %get-tuple-element.30), channel_id=1, source_target_pairs={{0,16},{1,17},{2,18},{3,19},{4,20},{5,21},{6,22},{7,23},{8,24},{9,... | collective-permute-start | bytes 786440 | tf_op jit(solution)/shard_map/ppermute | solution.py:28
  130.1 6.0 %collective-permute-done.21.came = bf16[2,128,512]{2,1,0:T(8,128)(2,1)S(1)} collective-permute-done((bf16[2,128,512]{2,1,0:T(8,128)(2,1)S(1)}, bf16[2,128,512]{2,1,0:T(8,128)(2,1)S(1)}, u32[]{:S(2)}, u32[]{:S(2)}) %collective-permute-start.21) | collective-permute-done | bytes 262176 | tf_op jit(solution)/shard_map/ppermute | solution.py:28
  137.9 1.9 %collective-permute-start.22 = (bf16[128,512]{1,0:T(8,128)(2,1)S(1)}, bf16[128,512]{1,0:T(8,128)(2,1)S(1)}, u32[]{:S(2)}, u32[]{:S(2)}) collective-permute-start(bf16[128,512]{1,0:T(8,128)(2,1)S(1)} %get-tuple-element.33), channel_id=1, source_target_pairs={{0,32},{1,33},{2,34},{3,35},{4,36},{5,37},{6,38},{7,39},{8,40},{9,... | collective-permute-start | bytes 393224 | tf_op jit(solution)/shard_map/ppermute | solution.py:28
  139.8 12.3 %all_to_all.15.share = bf16[8,8,512]{2,1,0:T(8,128)(2,1)S(1)} all-to-all(bf16[8,8,512]{2,1,0:T(8,128)(2,1)S(1)} %get-tuple-element.31), channel_id=1, replica_groups=mesh['z'=8,'y'=4,'x'=4,'h'=2,'k'=2] {'y','h'}, dimensions={0} | all-to-all | bytes 131072 | tf_op jit(solution)/shard_map/all_to_all | solution.py:259
  153.1 16.7 %all_to_all.16.own = bf16[32,8,512]{2,1,0:T(8,128)(2,1)S(1)} all-to-all(bf16[32,8,512]{2,1,0:T(8,128)(2,1)S(1)} %get-tuple-element.35), channel_id=1, replica_groups=mesh['z'=8,'y'=4,'x'=4,'h'=2,'k'=2] {'z','x'}, dimensions={0} | all-to-all | bytes 524288 | tf_op jit(solution)/shard_map/all_to_all | solution.py:266
  169.8 6.7 %collective-permute-start.23 = (bf16[32,8,512]{2,1,0:T(8,128)(2,1)S(1)}, bf16[32,8,512]{2,1,0:T(8,128)(2,1)S(1)}, u32[]{:S(2)}, u32[]{:S(2)}) collective-permute-start(bf16[32,8,512]{2,1,0:T(8,128)(2,1)S(1)} %all_to_all.16.own), channel_id=1, source_target_pairs={{0,1},{1,0},{2,3},{3,2},{4,5},{5,4},{6,7},{7,6},{8,9},{9,8},{10,11... | collective-permute-start | bytes 786440 | tf_op jit(solution)/shard_map/ppermute | solution.py:28
  (44 shorter events, 15.6 us)
Async XLA Ops:
  1.7 19.5 %collective-permute-start.6 = (bf16[128,512]{1,0:T(8,128)(2,1)S(1)}, bf16[128,512]{1,0:T(8,128)(2,1)S(1)}, u32[]{:S(2)}, u32[]{:S(2)}) collective-permute-start(bf16[128,512]{1,0:T(8,128)(2,1)S(1)} %multiply_convert_fusion), channel_id=1, source_target_pairs={{0,2},{1,3},{2,0},{3,1},{4,6},{5,7},{6,4},{7,5},{8,10},{9,11},{10,... | collective-permute-start | bytes 393224 | tf_op jit(solution)/shard_map/ppermute | solution.py:28
  9.9 15.9 %collective-permute-start.4 = (bf16[128,512]{1,0:T(8,128)(2,1)S(1)}, bf16[128,512]{1,0:T(8,128)(2,1)S(1)}, u32[]{:S(2)}, u32[]{:S(2)}) collective-permute-start(bf16[128,512]{1,0:T(8,128)(2,1)S(1)} %multiply_convert_fusion), channel_id=1, source_target_pairs={{0,8},{1,9},{2,10},{3,11},{4,12},{5,13},{6,14},{7,15},{8,0},{9,1},... | collective-permute-start | bytes 393224 | tf_op jit(solution)/shard_map/ppermute | solution.py:28
  14.6 13.8 %collective-permute-start.5 = (bf16[128,512]{1,0:T(8,128)(2,1)S(1)}, bf16[128,512]{1,0:T(8,128)(2,1)S(1)}, u32[]{:S(2)}, u32[]{:S(2)}) collective-permute-start(bf16[128,512]{1,0:T(8,128)(2,1)S(1)} %multiply_convert_fusion), channel_id=1, source_target_pairs={{0,4},{1,5},{2,6},{3,7},{4,8},{5,9},{6,10},{7,11},{8,12},{9,13},{1... | collective-permute-start | bytes 393224 | tf_op jit(solution)/shard_map/ppermute | solution.py:28
  16.8 11.5 %collective-permute-start.3 = (bf16[128,512]{1,0:T(8,128)(2,1)S(1)}, bf16[128,512]{1,0:T(8,128)(2,1)S(1)}, u32[]{:S(2)}, u32[]{:S(2)}) collective-permute-start(bf16[128,512]{1,0:T(8,128)(2,1)S(1)} %multiply_convert_fusion), channel_id=1, source_target_pairs={{0,12},{1,13},{2,14},{3,15},{4,0},{5,1},{6,2},{7,3},{8,4},{9,5},{1... | collective-permute-start | bytes 393224 | tf_op jit(solution)/shard_map/ppermute | solution.py:28
  21.1 11.6 %collective-permute-start.7 = (bf16[128,512]{1,0:T(8,128)(2,1)S(1)}, bf16[128,512]{1,0:T(8,128)(2,1)S(1)}, u32[]{:S(2)}, u32[]{:S(2)}) collective-permute-start(bf16[128,512]{1,0:T(8,128)(2,1)S(1)} %collective-permute-done.6), channel_id=1, source_target_pairs={{0,12},{1,13},{2,14},{3,15},{4,0},{5,1},{6,2},{7,3},{8,4},{9,5},{1... | collective-permute-start | bytes 393224 | tf_op jit(solution)/shard_map/ppermute | solution.py:28
  23.0 9.7 %collective-permute-start.8 = (bf16[128,512]{1,0:T(8,128)(2,1)S(1)}, bf16[128,512]{1,0:T(8,128)(2,1)S(1)}, u32[]{:S(2)}, u32[]{:S(2)}) collective-permute-start(bf16[128,512]{1,0:T(8,128)(2,1)S(1)} %collective-permute-done.6), channel_id=1, source_target_pairs={{0,8},{1,9},{2,10},{3,11},{4,12},{5,13},{6,14},{7,15},{8,0},{9,1},... | collective-permute-start | bytes 393224 | tf_op jit(solution)/shard_map/ppermute | solution.py:28
  25.9 8.1 %collective-permute-start.9 = (bf16[128,512]{1,0:T(8,128)(2,1)S(1)}, bf16[128,512]{1,0:T(8,128)(2,1)S(1)}, u32[]{:S(2)}, u32[]{:S(2)}) collective-permute-start(bf16[128,512]{1,0:T(8,128)(2,1)S(1)} %collective-permute-done.6), channel_id=1, source_target_pairs={{0,4},{1,5},{2,6},{3,7},{4,8},{5,9},{6,10},{7,11},{8,12},{9,13},{1... | collective-permute-start | bytes 393224 | tf_op jit(solution)/shard_map/ppermute | solution.py:28
  28.5 11.3 %collective-permute-start.10 = (bf16[4,128,512]{2,1,0:T(8,128)(2,1)S(1)}, bf16[4,128,512]{2,1,0:T(8,128)(2,1)S(1)}, u32[]{:S(2)}, u32[]{:S(2)}) collective-permute-start(bf16[4,128,512]{2,1,0:T(8,128)(2,1)S(1)} %pad_maximum_fusion.own), channel_id=1, source_target_pairs={{0,1},{1,0},{2,3},{3,2},{4,5},{5,4},{6,7},{7,6},{8,9},{9,8},{10,11... | collective-permute-start | bytes 1572872 | tf_op jit(solution)/shard_map/ppermute | solution.py:28
  34.0 5.8 %collective-permute-start.11 = (bf16[4,128,512]{2,1,0:T(8,128)(2,1)S(1)}, bf16[4,128,512]{2,1,0:T(8,128)(2,1)S(1)}, u32[]{:S(2)}, u32[]{:S(2)}) collective-permute-start(bf16[4,128,512]{2,1,0:T(8,128)(2,1)S(1)} %pad_maximum_fusion.1.own_h), channel_id=1, source_target_pairs={{0,1},{1,0},{2,3},{3,2},{4,5},{5,4},{6,7},{7,6},{8,9},{9,8},{10,11... | collective-permute-start | bytes 1572872 | tf_op jit(solution)/shard_map/ppermute | solution.py:28
  39.8 0.8 copy-start.2
  40.6 26.6 %copy-start.1 = (bf16[128,512]{1,0:T(8,128)(2,1)S(1)}, bf16[128,512]{1,0:T(8,128)(2,1)}, u32[]{:S(2)}) copy-start(bf16[128,512]{1,0:T(8,128)(2,1)} %features.1) | copy-start | bytes 393220
  45.5 15.0 %collective-permute-start.12 = (bf16[4,64,512]{2,1,0:T(8,128)(2,1)S(1)}, bf16[4,64,512]{2,1,0:T(8,128)(2,1)S(1)}, u32[]{:S(2)}, u32[]{:S(2)}) collective-permute-start(bf16[4,64,512]{2,1,0:T(8,128)(2,1)S(1)} %get-tuple-element.23), channel_id=1, source_target_pairs={{0,64},{1,65},{2,66},{3,67},{4,68},{5,69},{6,70},{7,71},{8,72},{9,... | collective-permute-start | bytes 786440 | tf_op jit(solution)/shard_map/ppermute | solution.py:28
  48.6 13.9 %collective-permute-start.16 = (bf16[4,64,512]{2,1,0:T(8,128)(2,1)S(1)}, bf16[4,64,512]{2,1,0:T(8,128)(2,1)S(1)}, u32[]{:S(2)}, u32[]{:S(2)}) collective-permute-start(bf16[4,64,512]{2,1,0:T(8,128)(2,1)S(1)} %get-tuple-element.27), channel_id=1, source_target_pairs={{0,448},{1,449},{2,450},{3,451},{4,452},{5,453},{6,454},{7,455},{8... | collective-permute-start | bytes 786440 | tf_op jit(solution)/shard_map/ppermute | solution.py:28
  60.6 14.5 %collective-permute-start.13 = (bf16[4,128,512]{2,1,0:T(8,128)(2,1)S(1)}, bf16[4,128,512]{2,1,0:T(8,128)(2,1)S(1)}, u32[]{:S(2)}, u32[]{:S(2)}) collective-permute-start(bf16[4,128,512]{2,1,0:T(8,128)(2,1)S(1)} %ring_add.6), channel_id=1, source_target_pairs={{0,64},{1,65},{2,66},{3,67},{4,68},{5,69},{6,70},{7,71},{8,72},{9,... | collective-permute-start | bytes 1572872 | tf_op jit(solution)/shard_map/ppermute | solution.py:28
  62.6 14.6 %collective-permute-start.17 = (bf16[4,128,512]{2,1,0:T(8,128)(2,1)S(1)}, bf16[4,128,512]{2,1,0:T(8,128)(2,1)S(1)}, u32[]{:S(2)}, u32[]{:S(2)}) collective-permute-start(bf16[4,128,512]{2,1,0:T(8,128)(2,1)S(1)} %ring_add.9), channel_id=1, source_target_pairs={{0,448},{1,449},{2,450},{3,451},{4,452},{5,453},{6,454},{7,455},{8... | collective-permute-start | bytes 1572872 | tf_op jit(solution)/shard_map/ppermute | solution.py:28
  67.2 10.0 %collective-permute-start = (bf16[128,512]{1,0:T(8,128)(2,1)S(1)}, bf16[128,512]{1,0:T(8,128)(2,1)S(1)}, u32[]{:S(2)}, u32[]{:S(2)}) collective-permute-start(bf16[128,512]{1,0:T(8,128)(2,1)S(1)} %copy-done.1), channel_id=1, source_target_pairs={{0,48},{1,49},{2,50},{3,51},{4,52},{5,53},{6,54},{7,55},{8,56},{9,... | collective-permute-start | bytes 393224 | tf_op jit(solution)/shard_map/ppermute | solution.py:28
  75.2 14.3 %collective-permute-start.14 = (bf16[4,128,512]{2,1,0:T(8,128)(2,1)S(1)}, bf16[4,128,512]{2,1,0:T(8,128)(2,1)S(1)}, u32[]{:S(2)}, u32[]{:S(2)}) collective-permute-start(bf16[4,128,512]{2,1,0:T(8,128)(2,1)S(1)} %ring_add.7), channel_id=1, source_target_pairs={{0,64},{1,65},{2,66},{3,67},{4,68},{5,69},{6,70},{7,71},{8,72},{9,... | collective-permute-start | bytes 1572872 | tf_op jit(solution)/shard_map/ppermute | solution.py:28
  77.3 15.1 %collective-permute-start.18 = (bf16[4,128,512]{2,1,0:T(8,128)(2,1)S(1)}, bf16[4,128,512]{2,1,0:T(8,128)(2,1)S(1)}, u32[]{:S(2)}, u32[]{:S(2)}) collective-permute-start(bf16[4,128,512]{2,1,0:T(8,128)(2,1)S(1)} %ring_add.10), channel_id=1, source_target_pairs={{0,448},{1,449},{2,450},{3,451},{4,452},{5,453},{6,454},{7,455},{8... | collective-permute-start | bytes 1572872 | tf_op jit(solution)/shard_map/ppermute | solution.py:28
  82.0 10.4 %collective-permute-start.1 = (bf16[128,512]{1,0:T(8,128)(2,1)S(1)}, bf16[128,512]{1,0:T(8,128)(2,1)S(1)}, u32[]{:S(2)}, u32[]{:S(2)}) collective-permute-start(bf16[128,512]{1,0:T(8,128)(2,1)S(1)} %copy-done.1), channel_id=1, source_target_pairs={{0,32},{1,33},{2,34},{3,35},{4,36},{5,37},{6,38},{7,39},{8,40},{9,... | collective-permute-start | bytes 393224 | tf_op jit(solution)/shard_map/ppermute | solution.py:28
  89.6 14.6 %collective-permute-start.15 = (bf16[4,128,512]{2,1,0:T(8,128)(2,1)S(1)}, bf16[4,128,512]{2,1,0:T(8,128)(2,1)S(1)}, u32[]{:S(2)}, u32[]{:S(2)}) collective-permute-start(bf16[4,128,512]{2,1,0:T(8,128)(2,1)S(1)} %ring_add.8), channel_id=1, source_target_pairs={{0,64},{1,65},{2,66},{3,67},{4,68},{5,69},{6,70},{7,71},{8,72},{9,... | collective-permute-start | bytes 1572872 | tf_op jit(solution)/shard_map/ppermute | solution.py:28
  92.5 59.6 %copy-start = (bf16[512,512]{1,0:T(8,128)(2,1)S(1)}, bf16[512,512]{1,0:T(8,128)(2,1)}, u32[]{:S(2)}) copy-start(bf16[512,512]{1,0:T(8,128)(2,1)} %weight.1) | copy-start | bytes 1572868
  92.5 12.9 %collective-permute-start.19 = (bf16[4,128,512]{2,1,0:T(8,128)(2,1)S(1)}, bf16[4,128,512]{2,1,0:T(8,128)(2,1)S(1)}, u32[]{:S(2)}, u32[]{:S(2)}) collective-permute-start(bf16[4,128,512]{2,1,0:T(8,128)(2,1)S(1)} %ring_add.11), channel_id=1, source_target_pairs={{0,448},{1,449},{2,450},{3,451},{4,452},{5,453},{6,454},{7,455},{8... | collective-permute-start | bytes 1572872 | tf_op jit(solution)/shard_map/ppermute | solution.py:28
  97.1 8.5 %collective-permute-start.2 = (bf16[128,512]{1,0:T(8,128)(2,1)S(1)}, bf16[128,512]{1,0:T(8,128)(2,1)S(1)}, u32[]{:S(2)}, u32[]{:S(2)}) collective-permute-start(bf16[128,512]{1,0:T(8,128)(2,1)S(1)} %copy-done.1), channel_id=1, source_target_pairs={{0,16},{1,17},{2,18},{3,19},{4,20},{5,21},{6,22},{7,23},{8,24},{9,... | collective-permute-start | bytes 393224 | tf_op jit(solution)/shard_map/ppermute | solution.py:28
  107.0 6.9 %collective-permute-start.20 = (bf16[256,512]{1,0:T(8,128)(2,1)S(1)}, bf16[256,512]{1,0:T(8,128)(2,1)S(1)}, u32[]{:S(2)}, u32[]{:S(2)}) collective-permute-start(bf16[256,512]{1,0:T(8,128)(2,1)S(1)} %get-tuple-element.29), channel_id=1, source_target_pairs={{0,1},{1,0},{2,3},{3,2},{4,5},{5,4},{6,7},{7,6},{8,9},{9,8},{10,11... | collective-permute-start | bytes 786440 | tf_op jit(solution)/shard_map/ppermute | solution.py:28
  114.6 22.7 %all-to-all-start = ((bf16[32,8,512]{2,1,0:T(8,128)(2,1)}), bf16[32,8,512]{2,1,0:T(8,128)(2,1)S(1)}, u32[]{:S(2)}, u32[]{:S(2)}) async-start(bf16[32,8,512]{2,1,0:T(8,128)(2,1)} %weight_half.1), calls=%async_computation | async-start | bytes 524288 | tf_op jit(solution)/shard_map/all_to_all | solution.py:247
  125.7 10.5 %collective-permute-start.21 = (bf16[2,128,512]{2,1,0:T(8,128)(2,1)S(1)}, bf16[2,128,512]{2,1,0:T(8,128)(2,1)S(1)}, u32[]{:S(2)}, u32[]{:S(2)}) collective-permute-start(bf16[2,128,512]{2,1,0:T(8,128)(2,1)S(1)} %get-tuple-element.30), channel_id=1, source_target_pairs={{0,16},{1,17},{2,18},{3,19},{4,20},{5,21},{6,22},{7,23},{8,24},{9,... | collective-permute-start | bytes 786440 | tf_op jit(solution)/shard_map/ppermute | solution.py:28
  137.9 14.2 %collective-permute-start.22 = (bf16[128,512]{1,0:T(8,128)(2,1)S(1)}, bf16[128,512]{1,0:T(8,128)(2,1)S(1)}, u32[]{:S(2)}, u32[]{:S(2)}) collective-permute-start(bf16[128,512]{1,0:T(8,128)(2,1)S(1)} %get-tuple-element.33), channel_id=1, source_target_pairs={{0,32},{1,33},{2,34},{3,35},{4,36},{5,37},{6,38},{7,39},{8,40},{9,... | collective-permute-start | bytes 393224 | tf_op jit(solution)/shard_map/ppermute | solution.py:28
  169.8 7.9 %collective-permute-start.23 = (bf16[32,8,512]{2,1,0:T(8,128)(2,1)S(1)}, bf16[32,8,512]{2,1,0:T(8,128)(2,1)S(1)}, u32[]{:S(2)}, u32[]{:S(2)}) collective-permute-start(bf16[32,8,512]{2,1,0:T(8,128)(2,1)S(1)} %all_to_all.16.own), channel_id=1, source_target_pairs={{0,1},{1,0},{2,3},{3,2},{4,5},{5,4},{6,7},{7,6},{8,9},{9,8},{10,11... | collective-permute-start | bytes 786440 | tf_op jit(solution)/shard_map/ppermute | solution.py:28
